TPU v7x, 1024 devices: a whole 8x8x8 slice. The times are simulated.
1024 devices in a mesh: mx: 64 (over x, y), my: 16 (over z, core).
Axes of the slice: x: 8, y: 8, z: 8, core: 2. Of those that a mesh axis runs over, the one named last changes fastest.
Arguments:
- tokens: bfloat16 [2048, 18432], P('mx', 'my'), may hold values from -6 to 6
- q_weight: bfloat16 [18432, 12288], P('my', 'mx'), may hold values from -0.046875 to 0.046875
- kv_weight: bfloat16 [18432, 512], P('my'), may hold values from -0.046875 to 0.046875
- key_cache: bfloat16 [2048, 1024, 256], P(('mx', 'my')), may hold values from -450 to 450
- value_cache: bfloat16 [2048, 1024, 256], P(('mx', 'my')), may hold values from -6 to 6
- lengths: int32 [2048], P(('mx', 'my')), may hold values from 1 to 1024, 1048576 in all
Outputs:
- attended: bfloat16 [2048, 12288], P(('mx', 'my'))
Inputs may be any that keep to these rules, and one draw needn't show every extreme that they name: lengths[r] slots of row r hold cached tokens; some row has all 1024.
All inputs are finite; a program needn't handle non-finite values. No bound on the sum of `lengths` on one device may be relied on, other than what follows from the above.
Results may differ from a plain program's by a relative error of at most 0.022.
Values may be sent and summed in bfloat16 or wider, within the bound.
No kernel may reach another device: no remote copies, remote signals or barrier semaphores. Data moves between devices by JAX's collectives and lax.ppermute only.
A program may use at most 32 MiB of HBM per device.

v0:
```python
import math

import jax
import jax.numpy as jnp
from jax import lax
from jax.sharding import PartitionSpec as P


def local(tokens, q_weight, kv_weight, key_cache, value_cache, lengths):
    mx_count = lax.axis_size("mx")
    my_count = lax.axis_size("my")
    local_rows = tokens.shape[0]
    own_rows = local_rows // my_count
    columns = q_weight.shape[1]
    head_size = key_cache.shape[2]
    slot_count = key_cache.shape[1]
    new_partial = jnp.dot(tokens, kv_weight, preferred_element_type=jnp.float32)
    gathered = lax.all_gather(tokens, "mx", axis=0, tiled=True)
    partial_value = jnp.dot(gathered, q_weight, preferred_element_type=jnp.float32)
    partial_value = partial_value.reshape(mx_count, my_count, own_rows, columns)
    summed, new_sums = (
        lax.psum_scatter(partial_value, "my", scatter_dimension=1, tiled=True),
        lax.psum_scatter(new_partial, "my", scatter_dimension=0, tiled=True),
    )
    query_block = summed.astype(jnp.bfloat16)
    query_rows = lax.all_to_all(query_block, "mx", split_axis=0, concat_axis=3, tiled=True)
    queries = query_rows.reshape(own_rows, -1, head_size)
    new_pairs = new_sums.astype(jnp.bfloat16)
    new_key = new_pairs[:, :head_size]
    new_value = new_pairs[:, head_size:]
    scale_factor = 1.0 / math.sqrt(head_size)
    scores = (
        jnp.einsum("rhd,rcd->rhc", queries, key_cache, preferred_element_type=jnp.float32)
        * scale_factor
    )
    own_score = (
        jnp.einsum("rhd,rd->rh", queries, new_key, preferred_element_type=jnp.float32)
        * scale_factor
    )
    slot_index = lax.broadcasted_iota(jnp.int32, (1, 1, slot_count), 2)
    live_mask = slot_index < lengths[:, None, None]
    peak_score = jnp.maximum(jnp.max(jnp.where(live_mask, scores, -jnp.inf), axis=2), own_score)
    raw_weights = jnp.where(live_mask, jnp.exp(scores - peak_score[:, :, None]), 0.0)
    own_raw = jnp.exp(own_score - peak_score)
    totals = jnp.sum(raw_weights, axis=2) + own_raw
    weights = (raw_weights / totals[:, :, None]).astype(jnp.bfloat16)
    own_weight = (own_raw / totals).astype(jnp.bfloat16)
    blended = jnp.einsum("rhc,rcd->rhd", weights, value_cache, preferred_element_type=jnp.float32)
    blended = (
        blended
        + own_weight.astype(jnp.float32)[:, :, None] * new_value.astype(jnp.float32)[:, None, :]
    )
    return blended.astype(jnp.bfloat16).reshape(own_rows, -1)


def solution(mesh):
    return jax.shard_map(
        local,
        mesh=mesh,
        in_specs=(
            P("mx", "my"),
            P("my", "mx"),
            P("my", None),
            P(("mx", "my"), None, None),
            P(("mx", "my"), None, None),
            P(("mx", "my")),
        ),
        out_specs=P(("mx", "my"), None),
        check_vma=False,
    )
```

profile of v0, /device:TPU:2, one launch (start us, length us, event | category | flops | bytes accessed | tf_op | source)
XLA Modules:
  0.0 225.7 jit_solution(16929112532442617589)
XLA Ops:
  6.5 0.0 copy-start
  6.5 0.0 all-gather.2.cloned.1.call-start
  6.5 0.7 all-gather.2.cloned.1.call-update
  7.3 0.0 reduce-scatter.2.cloned.1.call-start
  7.3 108.3 %all-gather.2.cloned.1.call-done = bf16[2048,1152]{1,0:T(8,128)(2,1)} async-done(((bf16[32,1152]{1,0:T(8,128)(2,1)}), bf16[2048,1152]{1,0:T(8,128)(2,1)}) %all-gather.2.cloned.1.call-update) | async-done | bytes 4718608 | tf_op jit(solution)/shard_map/all_gather | solution.py:18
  115.6 5.4 %fusion.12 = f32[2048,192]{1,0:T(8,128)} fusion(bf16[2048,1152]{1,0:T(8,128)(2,1)} %all-gather.2.cloned.1.call-done, bf16[1152,192]{0,1:T(8,128)(2,1)} %param.7), kind=kOutput, calls=%fused_computation.25 | convolution fusion | flops 905969664 | bytes 6733824 | tf_op jit(solution)/shard_map/dot_general | solution.py:19
  121.0 2.5 %reshape.35 = f32[64,16,2,192]{3,2,1,0:T(2,128)S(1)} reshape(f32[2048,192]{1,0:T(8,128)} %fusion.12) | data formatting | bytes 3145728 | tf_op jit(solution)/shard_map/reshape | solution.py:20
  123.5 2.5 %copy.13 = f32[64,16,2,192]{3,0,2,1:T(8,128)} copy(f32[64,16,2,192]{3,2,1,0:T(2,128)S(1)} %reshape.35) | data formatting | bytes 3145728 | tf_op jit(solution)/shard_map/reshape | solution.py:20
  126.0 0.0 copy-start.2
  126.0 0.0 copy-start.3
  126.0 0.0 copy-start.1
  126.0 0.0 reduce-scatter.2.cloned.1.call-update
  126.1 0.0 copy-start.4
  126.1 1.4 dynamic-slice
  128.2 0.0 copy-done
  128.2 0.0 copy-done.2
  128.2 0.3 fusion.13
  128.5 48.2 %all-reduce = bf16[32,512]{1,0:T(8,128)(2,1)S(1)} all-reduce(f32[32,512]{1,0:T(8,128)S(1)} %fusion.13), channel_id=3, replica_groups=mesh['mx'=64,'my'=16] {'my'}, use_global_device_ids=true, to_apply=%region_2.3.clone | all-reduce | flops 16384 | bytes 98304
  176.6 0.0 copy-done.3
  176.6 0.1 iota_compare_fusion
  176.7 14.4 %reduce-scatter.2.cloned.1.call-done = f32[64,1,2,192]{3,0,2,1:T(8,128)} async-done(((f32[64,16,2,192]{3,0,2,1:T(8,128)}), f32[64,1,2,192]{3,0,2,1:T(8,128)}) %reduce-scatter.2.cloned.1.call-update) | async-done | bytes 98320 | tf_op jit(solution)/shard_map/reduce_scatter | solution.py:22
  191.1 0.9 convert_element_type.21
  192.0 0.7 copy.14
  192.7 12.8 %all-to-all-start = ((bf16[64,1,2,192]{3,2,1,0:T(2,128)(2,1)}), bf16[64,1,2,192]{3,2,1,0:T(2,128)(2,1)S(1)}, u32[]{:S(2)}, u32[]{:S(2)}) async-start(bf16[64,1,2,192]{3,2,1,0:T(2,128)(2,1)} %copy.14), calls=%async_computation.1 | async-start | bytes 131072 | tf_op jit(solution)/shard_map/all_to_all | solution.py:26
  205.5 11.4 %all-to-all-done = bf16[64,1,2,192]{3,2,1,0:T(2,128)(2,1)S(1)} async-done(((bf16[64,1,2,192]{3,2,1,0:T(2,128)(2,1)}), bf16[64,1,2,192]{3,2,1,0:T(2,128)(2,1)S(1)}, u32[]{:S(2)}, u32[]{:S(2)}) %all-to-all-start) | async-done | bytes 49184 | tf_op jit(solution)/shard_map/all_to_all | solution.py:26
  216.8 0.1 reshape.36
  217.0 0.1 fusion.7
  217.1 0.0 copy-done.1
  217.1 0.5 select_reduce_fusion
  217.6 0.2 fusion.2
  217.9 0.0 copy-done.4
  217.9 0.4 fusion.1
  218.2 0.7 copy.19
  (5 shorter events, 0.0 us)
Async XLA Ops:
  6.5 121.6 %copy-start = (bf16[1152,512]{1,0:T(8,128)(2,1)S(1)}, bf16[1152,512]{1,0:T(8,128)(2,1)}, u32[]{:S(2)}) copy-start(bf16[1152,512]{1,0:T(8,128)(2,1)} %param.8) | copy-start | bytes 3538948
  6.5 109.1 %all-gather.2.cloned.1.call-start = ((), (), s32[]{:S(2)}) async-start(), calls=%async_computation.2 | async-start | bytes 4792320 | tf_op jit(solution)/shard_map/all_gather | solution.py:18
  7.3 183.8 %reduce-scatter.2.cloned.1.call-start = ((), (), s32[]{:S(2)}) async-start(), calls=%async_computation.3 | async-start | bytes 2228224 | tf_op jit(solution)/shard_map/reduce_scatter | solution.py:22
  126.0 2.1 copy-start.2
  126.0 50.6 %copy-start.3 = (s32[2]{0:T(128)S(1)}, s32[2]{0:T(128)}, u32[]{:S(2)}) copy-start(s32[2]{0:T(128)} %param.11) | copy-start | bytes 28
  126.0 91.1 %copy-start.1 = (bf16[2,1024,256]{2,1,0:T(8,128)(2,1)S(1)}, bf16[2,1024,256]{2,1,0:T(8,128)(2,1)}, u32[]{:S(2)}) copy-start(bf16[2,1024,256]{2,1,0:T(8,128)(2,1)} %param.9) | copy-start | bytes 3145732
  126.1 91.8 %copy-start.4 = (bf16[2,1024,256]{2,1,0:T(8,128)(2,1)S(1)}, bf16[2,1024,256]{2,1,0:T(8,128)(2,1)}, u32[]{:S(2)}) copy-start(bf16[2,1024,256]{2,1,0:T(8,128)(2,1)} %param.10) | copy-start | bytes 3145732
  192.7 24.1 %all-to-all-start = ((bf16[64,1,2,192]{3,2,1,0:T(2,128)(2,1)}), bf16[64,1,2,192]{3,2,1,0:T(2,128)(2,1)S(1)}, u32[]{:S(2)}, u32[]{:S(2)}) async-start(bf16[64,1,2,192]{3,2,1,0:T(2,128)(2,1)} %copy.14), calls=%async_computation.1 | async-start | bytes 131072 | tf_op jit(solution)/shard_map/all_to_all | solution.py:26
Sparse Core Ops, SparseCore 0:
  11.6 103.9 all-gather.1
  126.2 64.8 reduce-scatter.1
where the time goes:
time: 226 us
  waiting for transfers between devices  135 us (60%)
  blocking collectives  48.2 us (21%)
  between operations  14.1 us (6%)
  starting transfers between devices  12.8 us (6%)
  local copies, waits for them, and re-layouts  8.01 us (4%)
  matrix products  6.63 us (3%)
    all_gather x1, waiting for transfers between devices, local(): gathered = lax.all_gather(tokens, 'mx', axis=0, tiled=True)  108 us
    unnamed x1, blocking collectives  48.2 us
    reduce_scatter x1, waiting for transfers between devices, local(): lax.psum_scatter(partial_value, 'my', scatter_dimension=1, tiled=True)  14.4 us
    all_to_all x1, starting transfers between devices, local(): lax.all_to_all(query_block, 'mx', split_axis=0, concat_axis=3, tiled=True)  12.8 us
    all_to_all x1, waiting for transfers between devices, local(): lax.all_to_all(query_block, 'mx', split_axis=0, concat_axis=3, tiled=True)  11.4 us
    dot_general x1, matrix products, local(): jnp.dot(gathered, q_weight, preferred_element_type=jnp.float32)  5.36 us
    reshape x2, local copies, waits for them, and re-layouts, local(): partial_value = partial_value.reshape(mx_count, my_count, own_rows, columns)  5.06 us
  transfers between devices with their start and end apart: 3, of which 3 were waited for; matrix products, arithmetic and copies ran while one was open for 1% of the time, Pallas kernels for 0%

commit v1 on v0

--- a/solution.py
+++ b/solution.py
@@ -1,31 +1,174 @@
+import functools
 import math
 
 import jax
 import jax.numpy as jnp
 from jax import lax
+from jax.experimental import pallas as pl
+from jax.experimental.pallas import tpu as pltpu
 from jax.sharding import PartitionSpec as P
 
+SIDE = 8
+LANES = 128
+NEAR = 3
+FAR = SIDE - NEAR
+
+
+def times(rows, weights):
+    return lax.dot_general(
+        rows, weights, (((1,), (1,)), ((), ())), preferred_element_type=jnp.float32
+    )
+
+
+def near_body(rows_ref, below_ref, own_ref, above_ref, pair_ref, other_ref, same_ref, held):
+    at = 0
+    for piece in (below_ref, own_ref, above_ref, pair_ref):
+        held[at : at + piece.shape[0], :] = piece[...]
+        at += piece.shape[0]
+    half = rows_ref.shape[0] // 2
+    sums = times(rows_ref[...], held[...])
+    other_ref[...] = sums[:half]
+    same_ref[...] = sums[half:]
+
+
+def near_sums(rows, *pieces):
+    half, width = rows.shape[0] // 2, rows.shape[1]
+    columns = sum(piece.shape[0] for piece in pieces)
+    product = jax.ShapeDtypeStruct((half, columns), jnp.float32)
+    return pl.pallas_call(
+        near_body,
+        out_shape=[product, product],
+        scratch_shapes=[pltpu.VMEM((columns, width), jnp.bfloat16)],
+        compiler_params=pltpu.CompilerParams(vmem_limit_bytes=16 * 2**20),
+        cost_estimate=pl.CostEstimate(
+            flops=4 * half * width * columns,
+            bytes_accessed=2 * width * (2 * half + columns) + 8 * half * columns,
+            transcendentals=0,
+        ),
+        name="near_sums",
+    )(rows, *pieces)
+
+
+def far_body(blocks, y_ref, rows_ref, weights_ref, other_ref, same_ref, held, sems):
+    columns = weights_ref.shape[0] // SIDE
+    half = rows_ref.shape[0] // 2
+    copies = []
+    for at in range(FAR):
+        source = lax.rem(y_ref[0] + 2 + at, SIDE) * columns
+        copies.append(
+            pltpu.make_async_copy(
+                weights_ref.at[pl.ds(pl.multiple_of(source, columns), columns), :],
+                held.at[pl.ds(at * columns, columns), :],
+                sems.at[at],
+            )
+        )
+        copies[-1].start()
+    rest = held.shape[0] - FAR * columns
+    held[FAR * columns :, :] = jnp.zeros((rest, held.shape[1]), held.dtype)
+    waited, done = 0, 0
+    while done < blocks:
+        last = min(done + 3, blocks)
+        while waited < FAR and waited * columns < last * LANES:
+            copies[waited].wait()
+            waited += 1
+        sums = times(rows_ref[...], held[done * LANES : last * LANES, :])
+        for block in range(done, last):
+            lanes = slice((block - done) * LANES, (block - done + 1) * LANES)
+            place = pl.ds(block, half, stride=blocks)
+            other_ref[place, :] = sums[:half, lanes]
+            same_ref[place, :] = sums[half:, lanes]
+        done = last
+
+
+def far_sums(y_index, rows, weights):
+    half, width = rows.shape[0] // 2, rows.shape[1]
+    columns = weights.shape[0] // SIDE
+    blocks = -(-FAR * columns // LANES)
+    product = jax.ShapeDtypeStruct((half * blocks, LANES), jnp.float32)
+    in_vmem = pl.BlockSpec(memory_space=pltpu.VMEM)
+    return pl.pallas_call(
+        functools.partial(far_body, blocks),
+        in_specs=[
+            pl.BlockSpec(memory_space=pltpu.SMEM),
+            in_vmem,
+            pl.BlockSpec(memory_space=pltpu.HBM),
+        ],
+        out_specs=[in_vmem, in_vmem],
+        out_shape=[product, product],
+        scratch_shapes=[
+            pltpu.VMEM((blocks * LANES, width), jnp.bfloat16),
+            pltpu.SemaphoreType.DMA((FAR,)),
+        ],
+        compiler_params=pltpu.CompilerParams(vmem_limit_bytes=50 * 2**20),
+        cost_estimate=pl.CostEstimate(
+            flops=4 * half * width * blocks * LANES,
+            bytes_accessed=2 * width * (2 * half + FAR * columns) + 8 * half * blocks * LANES,
+            transcendentals=0,
+        ),
+        name="far_sums",
+    )(y_index.reshape(1), rows, weights)
+
+
+def shift_y(step):
+    return [
+        (SIDE * x + y, SIDE * x + (y + step) % SIDE) for x in range(SIDE) for y in range(SIDE)
+    ]
+
 
 def local(tokens, q_weight, kv_weight, key_cache, value_cache, lengths):
-    mx_count = lax.axis_size("mx")
     my_count = lax.axis_size("my")
-    local_rows = tokens.shape[0]
-    own_rows = local_rows // my_count
+    planes = my_count // 2
+    own_rows = tokens.shape[0] // my_count
+    width = tokens.shape[1]
     columns = q_weight.shape[1]
     head_size = key_cache.shape[2]
     slot_count = key_cache.shape[1]
-    new_partial = jnp.dot(tokens, kv_weight, preferred_element_type=jnp.float32)
-    gathered = lax.all_gather(tokens, "mx", axis=0, tiled=True)
-    partial_value = jnp.dot(gathered, q_weight, preferred_element_type=jnp.float32)
-    partial_value = partial_value.reshape(mx_count, my_count, own_rows, columns)
-    summed, new_sums = (
-        lax.psum_scatter(partial_value, "my", scatter_dimension=1, tiled=True),
-        lax.psum_scatter(new_partial, "my", scatter_dimension=0, tiled=True),
-    )
-    query_block = summed.astype(jnp.bfloat16)
-    query_rows = lax.all_to_all(query_block, "mx", split_axis=0, concat_axis=3, tiled=True)
+    x_index = lax.axis_index("mx") // SIDE
+    y_index = lax.axis_index("mx") % SIDE
+    core = lax.axis_index("my") % 2
+
+    x_rings = [[SIDE * x + y for x in range(SIDE)] for y in range(SIDE)]
+    y_rings = [[SIDE * x + y for y in range(SIDE)] for x in range(SIDE)]
+    core_pairs = [(i, i ^ 1) for i in range(my_count)]
+    plane_groups = [
+        [(SIDE * x + y) * my_count + 2 * plane + one for plane in range(planes) for x in range(SIDE)]
+        for y in range(SIDE)
+        for one in range(2)
+    ]
+
+    weights_here = lax.all_gather(q_weight, "mx", axis=1, tiled=True, axis_index_groups=y_rings)
+    below = lax.ppermute(q_weight, "mx", shift_y(1))
+    above = lax.ppermute(q_weight, "mx", shift_y(-1))
+    halves = tokens.reshape(planes, 2, own_rows, width).transpose(1, 0, 2, 3)
+    halves = jnp.where(core == 0, halves[::-1], halves)
+    halves = halves.reshape(-1, width)
+    gathered = lax.all_gather(halves, "mx", axis=0, tiled=True, axis_index_groups=x_rings)
+    pair_columns = kv_weight.shape[1] // SIDE
+    pair_weight = lax.dynamic_slice_in_dim(kv_weight, x_index * pair_columns, pair_columns, 1)
+
+    rows = gathered.reshape(SIDE, 2, planes, own_rows, width).transpose(1, 2, 0, 3, 4)
+    rows = rows.reshape(-1, width)
+
+    def exchange(other_sums, same_sums):
+        swapped = lax.ppermute(other_sums, "my", core_pairs)
+        chip_sums = (same_sums + swapped).reshape(planes * SIDE, -1, other_sums.shape[1])
+        parts = lax.all_to_all(
+            chip_sums, ("mx", "my"), split_axis=0, concat_axis=0, axis_index_groups=plane_groups
+        )
+        sums = jnp.sum(parts.reshape(planes, SIDE, *parts.shape[1:]), axis=0)
+        return sums.astype(jnp.bfloat16).reshape(SIDE, own_rows, -1)
+
+    near = exchange(*near_sums(rows, below.T, q_weight.T, above.T, pair_weight.T))
+    new_pairs = near[:, :, NEAR * columns :].transpose(1, 0, 2).reshape(own_rows, -1)
+    near = near[:, :, : NEAR * columns].transpose(1, 0, 2)
+    rows, near, new_pairs = lax.optimization_barrier((rows, near, new_pairs))
+    far = exchange(*far_sums(y_index, rows, weights_here.T))
+    far = far[:, :, : FAR * columns].transpose(1, 0, 2)
+    query_rows = jnp.concatenate([near, far], axis=2).reshape(own_rows, SIDE, SIDE, columns)
+    query_rows = jnp.concatenate([query_rows, query_rows], axis=2)
+    query_rows = lax.dynamic_slice_in_dim(query_rows, (SIDE + 1 - y_index) % SIDE, SIDE, 2)
     queries = query_rows.reshape(own_rows, -1, head_size)
-    new_pairs = new_sums.astype(jnp.bfloat16)
+
     new_key = new_pairs[:, :head_size]
     new_value = new_pairs[:, head_size:]
     scale_factor = 1.0 / math.sqrt(head_size)

time: 226 us -> 135 us (0.60)
  waiting for transfers between devices: 135 us -> 39.8 us
  starting transfers between devices: 12.8 us -> 30.9 us
  blocking collectives: 48.2 us -> 34.6 us
  matrix products: 6.63 us -> 0.98 us
  Pallas kernels: 0 us -> 3.64 us
    all_gather x1, waiting for transfers between devices: 108 us -> 0.02 us  [local(): lax.all_gather(q_weight, 'mx', axis=1, tiled=True, axis_index_groups=y_ri...]
    unnamed x1 -> x0, blocking collectives: 48.2 us -> none
    all_gather x0 -> x1, blocking collectives: none -> 34.6 us  [local(): lax.all_gather(halves, 'mx', axis=0, tiled=True, axis_index_groups=x_rings)]
    all_to_all x1 -> x2, waiting for transfers between devices: 11.4 us -> 35.6 us  [exchange(): lax.all_to_all(chip_sums, ('mx', 'my'), split_axis=0, concat_axis=0, axis...]
    reduce_scatter x1 -> x0, waiting for transfers between devices: 14.4 us -> none  [local(): lax.psum_scatter(partial_value, 'my', scatter_dimension=1, tiled=True)]
    ppermute x0 -> x4, starting transfers between devices: none -> 11.9 us  [the longest x1 4.5 us: local(): above = lax.ppermute(q_weight, 'mx', shift_y(-1))]
    all_to_all x1 -> x2, starting transfers between devices: 12.8 us -> 19 us  [exchange(): lax.all_to_all(chip_sums, ('mx', 'my'), split_axis=0, concat_axis=0, axis...]
    dot_general x2 -> x0, matrix products: 5.65 us -> none  [the longest x1 5.36 us: local(): jnp.dot(gathered, q_weight, preferred_element_type=jnp.float32)]
  transfers between devices with their start and end apart: 3 -> 7, of which waited for: 3 -> 4; matrix products, arithmetic and copies ran while one was open for 1% -> 6% of each run, Pallas kernels for 0% -> 1%
where the time goes in v1:
time: 135 us; the launch traced here: 134 us
  waiting for transfers between devices  39.8 us (29%)
  blocking collectives  34.6 us (26%)
  starting transfers between devices  30.9 us (23%)
  between operations  13.7 us (10%)
  local copies, waits for them, and re-layouts  8.85 us (7%)
  Pallas kernels  3.64 us (3%)
  other arithmetic  1.61 us (1%)
    all_to_all x2, waiting for transfers between devices, exchange(): lax.all_to_all(chip_sums, ('mx', 'my'), split_axis=0, concat_axis=0, axis...  35.6 us
    all_gather x1, blocking collectives, local(): lax.all_gather(halves, 'mx', axis=0, tiled=True, axis_index_groups=x_rings)  34.6 us
    all_to_all x2, starting transfers between devices, exchange(): lax.all_to_all(chip_sums, ('mx', 'my'), split_axis=0, concat_axis=0, axis...  19 us
    ppermute x1, starting transfers between devices, local(): above = lax.ppermute(q_weight, 'mx', shift_y(-1))  4.5 us
    ppermute x2, starting transfers between devices, exchange(): swapped = lax.ppermute(other_sums, 'my', core_pairs)  3.84 us
    ppermute x1, starting transfers between devices, local(): below = lax.ppermute(q_weight, 'mx', shift_y(1))  3.6 us
    ppermute x2, waiting for transfers between devices, exchange(): swapped = lax.ppermute(other_sums, 'my', core_pairs)  3.47 us
    pallas_call x1, Pallas kernels, far_sums(): pl.pallas_call(functools.partial(far_body, blocks), in_specs=[pl.BlockSpe...  2.95 us
  transfers between devices with their start and end apart: 7, of which 4 were waited for; matrix products, arithmetic and copies ran while one was open for 6% of the time, Pallas kernels for 1%

profile of v1, /device:TPU:2, one launch (start us, length us, event | category | flops | bytes accessed | tf_op | source)
XLA Modules:
  0.0 134.1 jit_solution(3250054760552726309)
XLA Ops:
  6.5 0.0 copy-start
  6.5 0.0 all-gather.2.cloned.1.call-start
  6.5 0.7 all-gather.2.cloned.1.call-update
  7.3 3.6 %collective-permute-start = (bf16[1152,192]{0,1:T(8,128)(2,1)}, bf16[1152,192]{0,1:T(8,128)(2,1)S(1)}, u32[]{:S(2)}, u32[]{:S(2)}) collective-permute-start(bf16[1152,192]{0,1:T(8,128)(2,1)} %param.7), channel_id=1, source_target_pairs={{0,16},{16,32},{32,48},{48,64},{64,80},{80,96},{96,112},{112,0},{1... | collective-permute-start | bytes 1327112 | tf_op jit(solution)/shard_map/ppermute | solution.py:140
  10.9 4.5 %collective-permute-start.1 = (bf16[1152,192]{0,1:T(8,128)(2,1)}, bf16[1152,192]{0,1:T(8,128)(2,1)S(1)}, u32[]{:S(2)}, u32[]{:S(2)}) collective-permute-start(bf16[1152,192]{0,1:T(8,128)(2,1)} %param.7), channel_id=1, source_target_pairs={{0,112},{16,0},{32,16},{48,32},{64,48},{80,64},{96,80},{112,96},{1... | collective-permute-start | bytes 1327112 | tf_op jit(solution)/shard_map/ppermute | solution.py:141
  15.4 0.9 reshape.67
  16.3 0.1 copy.28
  16.4 0.1 broadcast_select_fusion
  16.5 0.0 copy-done
  16.5 0.2 constant_dynamic-slice_fusion
  16.6 0.2 copy.22
  16.8 34.6 %all_gather.6 = bf16[256,1152]{1,0:T(8,128)(2,1)S(1)} all-gather(bf16[32,1152]{1,0:T(8,128)(2,1)S(1)} %reshape.68), channel_id=1, replica_groups={{0,128,256,384,512,640,768,896},{16,144,272,400,528,656,784,912},{32,16..., dimensions={0}, use_global_device_ids=true | all-gather | bytes 663552 | tf_op jit(solution)/shard_map/all_gather | solution.py:145
  51.5 1.0 reshape.69
  52.5 2.4 %copy.14 = bf16[2,8,8,2,1152]{4,3,2,1,0:T(2,128)(2,1)} copy(bf16[2,8,8,2,1152]{4,3,1,0,2:T(2,128)(2,1)} %bitcast.39) | data formatting | bytes 1179648 | tf_op jit(solution)/shard_map/transpose | solution.py:149
  54.9 2.0 %reshape.70.rows_ref = bf16[256,1152]{1,0:T(8,128)(2,1)S(1)} reshape(bf16[2,8,8,2,1152]{4,3,2,1,0:T(2,128)(2,1)} %copy.14) | data formatting | bytes 1179648 | tf_op jit(solution)/shard_map/reshape | solution.py:150
  56.8 0.0 collective-permute-done
  56.8 0.0 collective-permute-done.1
  56.9 0.0 copy-done.1
  56.9 0.7 near_sums.1
  57.6 1.9 %collective-permute-start.2 = (f32[128,640]{1,0:T(8,128)S(1)}, f32[128,640]{1,0:T(8,128)S(1)}, u32[]{:S(2)}, u32[]{:S(2)}) collective-permute-start(f32[128,640]{1,0:T(8,128)S(1)} %get-tuple-element.13), channel_id=1, source_target_pairs={{0,1},{1,0},{2,3},{3,2},{4,5},{5,4},{6,7},{7,6},{8,9},{9,8},{10,11... | collective-permute-start | bytes 983048 | tf_op jit(solution)/shard_map/ppermute | solution.py:153
  59.5 1.6 %collective-permute-done.2 = f32[128,640]{1,0:T(8,128)S(1)} collective-permute-done((f32[128,640]{1,0:T(8,128)S(1)}, f32[128,640]{1,0:T(8,128)S(1)}, u32[]{:S(2)}, u32[]{:S(2)}) %collective-permute-start.2) | collective-permute-done | bytes 327712 | tf_op jit(solution)/shard_map/ppermute | solution.py:153
  61.1 0.9 reshape.71
  62.0 13.6 %all-to-all-start = ((f32[64,2,640]{2,1,0:T(2,128)}), f32[64,2,640]{2,1,0:T(2,128)S(1)}, u32[]{:S(2)}, u32[]{:S(2)}) async-start(f32[64,2,640]{2,1,0:T(2,128)} %reshape.71), calls=%async_computation | async-start | bytes 655360 | tf_op jit(solution)/shard_map/all_to_all | solution.py:155
  75.7 15.8 %all-to-all-done = f32[64,2,640]{2,1,0:T(2,128)S(1)} async-done(((f32[64,2,640]{2,1,0:T(2,128)}), f32[64,2,640]{2,1,0:T(2,128)S(1)}, u32[]{:S(2)}, u32[]{:S(2)}) %all-to-all-start) | async-done | bytes 327712 | tf_op jit(solution)/shard_map/all_to_all | solution.py:155
  91.5 0.1 reduce_sum.27
  91.6 0.1 slice_bitcast_fusion.2
  91.7 0.1 reshape.73
  91.8 0.0 all-gather.2.cloned.1.call-done
  91.8 2.9 %far_sums.1 = (f32[1024,128]{1,0:T(8,128)S(1)}, f32[1024,128]{1,0:T(8,128)S(1)}) custom-call(s32[1]{0:T(128)} %bitcast.9.y_ref, bf16[256,1152]{1,0:T(8,128)(2,1)S(1)} %reshape.70.rows_ref, bf16[1536,1152]{1,0:T(8,128)(2,1)} %bitcast.38), custom_call_target="tpu_custom_call" | custom-call | flops 603979776 | bytes 3850240 | tf_op jit(solution)/shard_map/far_sums/pallas_call | solution.py:89
  94.8 1.9 %collective-permute-start.3 = (f32[1024,128]{1,0:T(8,128)S(1)}, f32[1024,128]{1,0:T(8,128)S(1)}, u32[]{:S(2)}, u32[]{:S(2)}) collective-permute-start(f32[1024,128]{1,0:T(8,128)S(1)} %get-tuple-element.17), channel_id=1, source_target_pairs={{0,1},{1,0},{2,3},{3,2},{4,5},{5,4},{6,7},{7,6},{8,9},{9,8},{10,11... | collective-permute-start | bytes 1572872 | tf_op jit(solution)/shard_map/ppermute | solution.py:153
  96.7 1.9 %collective-permute-done.3 = f32[1024,128]{1,0:T(8,128)S(1)} collective-permute-done((f32[1024,128]{1,0:T(8,128)S(1)}, f32[1024,128]{1,0:T(8,128)S(1)}, u32[]{:S(2)}, u32[]{:S(2)}) %collective-permute-start.3) | collective-permute-done | bytes 524320 | tf_op jit(solution)/shard_map/ppermute | solution.py:153
  98.6 0.9 add.33
  99.4 5.3 %all-to-all-start.1 = ((f32[64,16,128]{2,1,0:T(8,128)}), f32[64,16,128]{2,1,0:T(8,128)S(1)}, u32[]{:S(2)}, u32[]{:S(2)}) async-start(f32[64,16,128]{2,1,0:T(8,128)} %bitcast.11), calls=%async_computation.1 | async-start | bytes 1048576 | tf_op jit(solution)/shard_map/all_to_all | solution.py:155
  104.8 0.0 copy-done.3
  104.8 0.1 iota_compare_fusion
  104.9 19.8 %all-to-all-done.1 = f32[64,16,128]{2,1,0:T(8,128)S(1)} async-done(((f32[64,16,128]{2,1,0:T(8,128)}), f32[64,16,128]{2,1,0:T(8,128)S(1)}, u32[]{:S(2)}, u32[]{:S(2)}) %all-to-all-start.1) | async-done | bytes 524320 | tf_op jit(solution)/shard_map/all_to_all | solution.py:155
  124.8 0.1 pad_maximum_fusion
  124.9 0.1 reshape.77
  125.0 0.0 copy-start.4
  125.0 0.1 fusion.7
  125.1 0.1 reshape.78
  125.3 0.1 fusion.8
  125.4 0.0 copy-done.2
  125.4 0.5 select_reduce_fusion
  125.9 0.2 fusion.2
  126.1 0.1 copy-done.4
  126.2 0.3 fusion.1
  126.6 0.7 copy.24
  (14 shorter events, 0.2 us)
Async XLA Ops:
  6.5 9.9 %copy-start = (bf16[1152,512]{1,0:T(8,128)(2,1)S(1)}, bf16[1152,512]{1,0:T(8,128)(2,1)}, u32[]{:S(2)}) copy-start(bf16[1152,512]{1,0:T(8,128)(2,1)} %param.8) | copy-start | bytes 3538948
  6.5 85.3 %all-gather.2.cloned.1.call-start = ((), (), s32[]{:S(2)}) async-start(), calls=%async_computation.2 | async-start | bytes 3981312 | tf_op jit(solution)/shard_map/all_gather | solution.py:139
  7.3 49.6 %collective-permute-start = (bf16[1152,192]{0,1:T(8,128)(2,1)}, bf16[1152,192]{0,1:T(8,128)(2,1)S(1)}, u32[]{:S(2)}, u32[]{:S(2)}) collective-permute-start(bf16[1152,192]{0,1:T(8,128)(2,1)} %param.7), channel_id=1, source_target_pairs={{0,16},{16,32},{32,48},{48,64},{64,80},{80,96},{96,112},{112,0},{1... | collective-permute-start | bytes 1327112 | tf_op jit(solution)/shard_map/ppermute | solution.py:140
  10.9 46.0 %collective-permute-start.1 = (bf16[1152,192]{0,1:T(8,128)(2,1)}, bf16[1152,192]{0,1:T(8,128)(2,1)S(1)}, u32[]{:S(2)}, u32[]{:S(2)}) collective-permute-start(bf16[1152,192]{0,1:T(8,128)(2,1)} %param.7), channel_id=1, source_target_pairs={{0,112},{16,0},{32,16},{48,32},{64,48},{80,64},{96,80},{112,96},{1... | collective-permute-start | bytes 1327112 | tf_op jit(solution)/shard_map/ppermute | solution.py:141
  52.5 4.4 %copy-start.1 = (bf16[1152,192]{0,1:T(8,128)(2,1)S(1)}, bf16[1152,192]{0,1:T(8,128)(2,1)}, u32[]{:S(2)}) copy-start(bf16[1152,192]{0,1:T(8,128)(2,1)} %param.7) | copy-start | bytes 1327108
  57.6 3.5 %collective-permute-start.2 = (f32[128,640]{1,0:T(8,128)S(1)}, f32[128,640]{1,0:T(8,128)S(1)}, u32[]{:S(2)}, u32[]{:S(2)}) collective-permute-start(f32[128,640]{1,0:T(8,128)S(1)} %get-tuple-element.13), channel_id=1, source_target_pairs={{0,1},{1,0},{2,3},{3,2},{4,5},{5,4},{6,7},{7,6},{8,9},{9,8},{10,11... | collective-permute-start | bytes 983048 | tf_op jit(solution)/shard_map/ppermute | solution.py:153
  62.0 29.4 %all-to-all-start = ((f32[64,2,640]{2,1,0:T(2,128)}), f32[64,2,640]{2,1,0:T(2,128)S(1)}, u32[]{:S(2)}, u32[]{:S(2)}) async-start(f32[64,2,640]{2,1,0:T(2,128)} %reshape.71), calls=%async_computation | async-start | bytes 655360 | tf_op jit(solution)/shard_map/all_to_all | solution.py:155
  94.8 3.8 %collective-permute-start.3 = (f32[1024,128]{1,0:T(8,128)S(1)}, f32[1024,128]{1,0:T(8,128)S(1)}, u32[]{:S(2)}, u32[]{:S(2)}) collective-permute-start(f32[1024,128]{1,0:T(8,128)S(1)} %get-tuple-element.17), channel_id=1, source_target_pairs={{0,1},{1,0},{2,3},{3,2},{4,5},{5,4},{6,7},{7,6},{8,9},{9,8},{10,11... | collective-permute-start | bytes 1572872 | tf_op jit(solution)/shard_map/ppermute | solution.py:153
  98.6 6.2 %copy-start.3 = (s32[2]{0:T(128)S(1)}, s32[2]{0:T(128)}, u32[]{:S(2)}) copy-start(s32[2]{0:T(128)} %param.11) | copy-start | bytes 28
  99.4 26.0 %copy-start.2 = (bf16[2,1024,256]{2,1,0:T(8,128)(2,1)S(1)}, bf16[2,1024,256]{2,1,0:T(8,128)(2,1)}, u32[]{:S(2)}) copy-start(bf16[2,1024,256]{2,1,0:T(8,128)(2,1)} %param.9) | copy-start | bytes 3145732
  99.4 25.3 %all-to-all-start.1 = ((f32[64,16,128]{2,1,0:T(8,128)}), f32[64,16,128]{2,1,0:T(8,128)S(1)}, u32[]{:S(2)}, u32[]{:S(2)}) async-start(f32[64,16,128]{2,1,0:T(8,128)} %bitcast.11), calls=%async_computation.1 | async-start | bytes 1048576 | tf_op jit(solution)/shard_map/all_to_all | solution.py:155
  125.0 1.2 copy-start.4
Sparse Core Ops, SparseCore 0:
  10.0 65.0 all-gather.1

commit v2 on v1

--- a/solution.py
+++ b/solution.py
@@ -20,33 +20,54 @@
     )
 
 
-def near_body(rows_ref, below_ref, own_ref, above_ref, pair_ref, other_ref, same_ref, held):
+def near_body(
+    planes, own_rows, core_ref, gathered_ref, below_ref, own_ref, above_ref, pair_ref,
+    rows_ref, other_ref, same_ref, held,
+):
     at = 0
     for piece in (below_ref, own_ref, above_ref, pair_ref):
         held[at : at + piece.shape[0], :] = piece[...]
         at += piece.shape[0]
-    half = rows_ref.shape[0] // 2
-    sums = times(rows_ref[...], held[...])
+    count = gathered_ref.shape[0]
+    half = count // 2
+    row_bits, x_bits = own_rows.bit_length() - 1, SIDE.bit_length() - 1
+    plane_bits = planes.bit_length() - 1
+    into = lax.broadcasted_iota(jnp.int32, (count, 1), 0)
+    row = into & (own_rows - 1)
+    x = (into >> row_bits) & (SIDE - 1)
+    plane = (into >> (row_bits + x_bits)) & (planes - 1)
+    same = into >> (row_bits + x_bits + plane_bits)
+    core = jnp.where(same == 1, core_ref[0], 1 - core_ref[0])
+    source = (((((x << plane_bits) + plane) << 1) + core) << row_bits) + row
+    pick = lax.broadcasted_iota(jnp.int32, (count, count), 1) == source
+    pick = jnp.where(pick, 1.0, 0.0).astype(jnp.bfloat16)
+    rows = jnp.dot(pick, gathered_ref[...], preferred_element_type=jnp.float32)
+    rows = rows.astype(jnp.bfloat16)
+    rows_ref[...] = rows
+    sums = times(rows, held[...])
     other_ref[...] = sums[:half]
     same_ref[...] = sums[half:]
 
 
-def near_sums(rows, *pieces):
-    half, width = rows.shape[0] // 2, rows.shape[1]
+def near_sums(planes, own_rows, core, gathered, *pieces):
+    count, width = gathered.shape
     columns = sum(piece.shape[0] for piece in pieces)
-    product = jax.ShapeDtypeStruct((half, columns), jnp.float32)
+    product = jax.ShapeDtypeStruct((count // 2, columns), jnp.float32)
+    in_vmem = pl.BlockSpec(memory_space=pltpu.VMEM)
     return pl.pallas_call(
-        near_body,
-        out_shape=[product, product],
+        functools.partial(near_body, planes, own_rows),
+        in_specs=[pl.BlockSpec(memory_space=pltpu.SMEM)] + [in_vmem] * (1 + len(pieces)),
+        out_specs=[in_vmem] * 3,
+        out_shape=[jax.ShapeDtypeStruct(gathered.shape, gathered.dtype), product, product],
         scratch_shapes=[pltpu.VMEM((columns, width), jnp.bfloat16)],
         compiler_params=pltpu.CompilerParams(vmem_limit_bytes=16 * 2**20),
         cost_estimate=pl.CostEstimate(
-            flops=4 * half * width * columns,
-            bytes_accessed=2 * width * (2 * half + columns) + 8 * half * columns,
+            flops=2 * count * width * (columns + count),
+            bytes_accessed=2 * width * (2 * count + columns) + 4 * count * columns,
             transcendentals=0,
         ),
         name="near_sums",
-    )(rows, *pieces)
+    )(core.reshape(1), gathered, *pieces)
 
 
 def far_body(blocks, y_ref, rows_ref, weights_ref, other_ref, same_ref, held, sems):
@@ -139,30 +160,30 @@
     weights_here = lax.all_gather(q_weight, "mx", axis=1, tiled=True, axis_index_groups=y_rings)
     below = lax.ppermute(q_weight, "mx", shift_y(1))
     above = lax.ppermute(q_weight, "mx", shift_y(-1))
-    halves = tokens.reshape(planes, 2, own_rows, width).transpose(1, 0, 2, 3)
-    halves = jnp.where(core == 0, halves[::-1], halves)
-    halves = halves.reshape(-1, width)
-    gathered = lax.all_gather(halves, "mx", axis=0, tiled=True, axis_index_groups=x_rings)
+    gathered = lax.all_gather(tokens, "mx", axis=0, tiled=True, axis_index_groups=x_rings)
     pair_columns = kv_weight.shape[1] // SIDE
     pair_weight = lax.dynamic_slice_in_dim(kv_weight, x_index * pair_columns, pair_columns, 1)
 
-    rows = gathered.reshape(SIDE, 2, planes, own_rows, width).transpose(1, 2, 0, 3, 4)
-    rows = rows.reshape(-1, width)
-
-    def exchange(other_sums, same_sums):
+    def chip_sums(other_sums, same_sums):
         swapped = lax.ppermute(other_sums, "my", core_pairs)
-        chip_sums = (same_sums + swapped).reshape(planes * SIDE, -1, other_sums.shape[1])
+        return (same_sums + swapped).reshape(planes * SIDE, -1, other_sums.shape[1])
+
+    def exchange(sums):
         parts = lax.all_to_all(
-            chip_sums, ("mx", "my"), split_axis=0, concat_axis=0, axis_index_groups=plane_groups
+            sums, ("mx", "my"), split_axis=0, concat_axis=0, axis_index_groups=plane_groups
         )
         sums = jnp.sum(parts.reshape(planes, SIDE, *parts.shape[1:]), axis=0)
         return sums.astype(jnp.bfloat16).reshape(SIDE, own_rows, -1)
 
-    near = exchange(*near_sums(rows, below.T, q_weight.T, above.T, pair_weight.T))
+    rows, *near = near_sums(
+        planes, own_rows, core, gathered, below.T, q_weight.T, above.T, pair_weight.T
+    )
+    near = exchange(chip_sums(*near))
     new_pairs = near[:, :, NEAR * columns :].transpose(1, 0, 2).reshape(own_rows, -1)
     near = near[:, :, : NEAR * columns].transpose(1, 0, 2)
-    rows, near, new_pairs = lax.optimization_barrier((rows, near, new_pairs))
-    far = exchange(*far_sums(y_index, rows, weights_here.T))
+    far = chip_sums(*far_sums(y_index, rows, weights_here.T))
+    far, near, new_pairs = lax.optimization_barrier((far, near, new_pairs))
+    far = exchange(far)
     far = far[:, :, : FAR * columns].transpose(1, 0, 2)
     query_rows = jnp.concatenate([near, far], axis=2).reshape(own_rows, SIDE, SIDE, columns)
     query_rows = jnp.concatenate([query_rows, query_rows], axis=2)

time: 135 us -> 127 us (0.941)
  waiting for transfers between devices: 39.8 us -> 32.6 us
  local copies, waits for them, and re-layouts: 8.85 us -> 2.38 us
  starting transfers between devices: 30.9 us -> 36.1 us
    all_to_all x2, waiting for transfers between devices: 35.6 us -> 24.6 us  [exchange(): lax.all_to_all(sums, ('mx', 'my'), split_axis=0, concat_axis=0, axis_inde...]
    all_gather x1, waiting for transfers between devices: 0.02 us -> 5.73 us  [local(): lax.all_gather(q_weight, 'mx', axis=1, tiled=True, axis_index_groups=y_ri...]
    all_to_all x2, starting transfers between devices: 19 us -> 24.2 us  [exchange(): lax.all_to_all(sums, ('mx', 'my'), split_axis=0, concat_axis=0, axis_inde...]
    reshape x6 -> x1, local copies, waits for them, and re-layouts: 4.91 us -> 0.9 us  [chip_sums(): return (same_sums + swapped).reshape(planes * SIDE, -1, other_sums.shape[1])]
    transpose x1 -> x0, local copies, waits for them, and re-layouts: 2.36 us -> none  [local(): gathered.reshape(SIDE, 2, planes, own_rows, width).transpose(1, 2, 0, 3, 4)]
    ppermute x2, waiting for transfers between devices: 3.47 us -> 1.6 us  [chip_sums(): swapped = lax.ppermute(other_sums, 'my', core_pairs)]
  transfers between devices with their start and end apart: 7 -> 7, of which waited for: 4 -> 4; matrix products, arithmetic and copies ran while one was open for 6% -> 1% of each run, Pallas kernels for 1% -> 3%
where the time goes in v2:
time: 127 us
  starting transfers between devices  36.1 us (28%)
  blocking collectives  34.6 us (27%)
  waiting for transfers between devices  32.6 us (26%)
  between operations  13.6 us (11%)
  Pallas kernels  3.83 us (3%)
  local copies, waits for them, and re-layouts  2.38 us (2%)
  matrix products  2.22 us (2%)
  other arithmetic  1.53 us (1%)
    all_gather x1, blocking collectives, local(): lax.all_gather(tokens, 'mx', axis=0, tiled=True, axis_index_groups=x_rings)  34.6 us
    all_to_all x2, waiting for transfers between devices, exchange(): lax.all_to_all(sums, ('mx', 'my'), split_axis=0, concat_axis=0, axis_inde...  24.6 us
    all_to_all x2, starting transfers between devices, exchange(): lax.all_to_all(sums, ('mx', 'my'), split_axis=0, concat_axis=0, axis_inde...  24.2 us
    all_gather x1, waiting for transfers between devices, local(): lax.all_gather(q_weight, 'mx', axis=1, tiled=True, axis_index_groups=y_ri...  5.73 us
    ppermute x1, starting transfers between devices, local(): above = lax.ppermute(q_weight, 'mx', shift_y(-1))  4.49 us
    ppermute x2, starting transfers between devices, chip_sums(): swapped = lax.ppermute(other_sums, 'my', core_pairs)  3.84 us
    ppermute x1, starting transfers between devices, local(): below = lax.ppermute(q_weight, 'mx', shift_y(1))  3.6 us
    pallas_call x1, Pallas kernels, far_sums(): pl.pallas_call(functools.partial(far_body, blocks), in_specs=[pl.BlockSpe...  2.94 us
  transfers between devices with their start and end apart: 7, of which 4 were waited for; matrix products, arithmetic and copies ran while one was open for 1% of the time, Pallas kernels for 3%

profile of v2, /device:TPU:2, one launch (start us, length us, event | category | flops | bytes accessed | tf_op | source)
XLA Modules:
  0.0 126.9 jit_solution(14491752901980476142)
XLA Ops:
  6.5 0.0 copy-start
  6.5 0.0 copy-start.1
  6.5 0.0 copy-start.3
  6.5 0.0 all-gather.2.cloned.1.call-start
  6.5 0.7 all-gather.2.cloned.1.call-update
  7.3 3.6 %collective-permute-start = (bf16[1152,192]{0,1:T(8,128)(2,1)}, bf16[1152,192]{0,1:T(8,128)(2,1)S(1)}, u32[]{:S(2)}, u32[]{:S(2)}) collective-permute-start(bf16[1152,192]{0,1:T(8,128)(2,1)} %param.7), channel_id=1, source_target_pairs={{0,16},{16,32},{32,48},{48,64},{64,80},{80,96},{96,112},{112,0},{1... | collective-permute-start | bytes 1327112 | tf_op jit(solution)/shard_map/ppermute | solution.py:161
  10.9 4.5 %collective-permute-start.1 = (bf16[1152,192]{0,1:T(8,128)(2,1)}, bf16[1152,192]{0,1:T(8,128)(2,1)S(1)}, u32[]{:S(2)}, u32[]{:S(2)}) collective-permute-start(bf16[1152,192]{0,1:T(8,128)(2,1)} %param.7), channel_id=1, source_target_pairs={{0,112},{16,0},{32,16},{48,32},{64,48},{80,64},{96,80},{112,96},{1... | collective-permute-start | bytes 1327112 | tf_op jit(solution)/shard_map/ppermute | solution.py:162
  15.4 0.0 copy-done
  15.4 0.1 constant_dynamic-slice_fusion
  15.6 0.2 copy.18
  15.7 0.0 copy-done.3
  15.8 34.6 %all_gather.6.gathered_ref = bf16[256,1152]{1,0:T(8,128)(2,1)S(1)} all-gather(bf16[32,1152]{1,0:T(8,128)(2,1)S(1)} %copy-done.3), channel_id=1, replica_groups={{0,128,256,384,512,640,768,896},{16,144,272,400,528,656,784,912},{32,16..., dimensions={0}, use_global_device_ids=true | all-gather | bytes 663552 | tf_op jit(solution)/shard_map/all_gather | solution.py:163
  50.4 0.0 collective-permute-done
  50.4 0.0 collective-permute-done.1
  50.4 0.0 copy-done.1
  50.4 0.9 near_sums.1
  51.3 1.9 %collective-permute-start.3 = (f32[128,640]{1,0:T(8,128)S(1)}, f32[128,640]{1,0:T(8,128)S(1)}, u32[]{:S(2)}, u32[]{:S(2)}) collective-permute-start(f32[128,640]{1,0:T(8,128)S(1)} %get-tuple-element.17), channel_id=1, source_target_pairs={{0,1},{1,0},{2,3},{3,2},{4,5},{5,4},{6,7},{7,6},{8,9},{9,8},{10,11... | collective-permute-start | bytes 983048 | tf_op jit(solution)/shard_map/ppermute | solution.py:168
  53.2 1.6 %collective-permute-done.3 = f32[128,640]{1,0:T(8,128)S(1)} collective-permute-done((f32[128,640]{1,0:T(8,128)S(1)}, f32[128,640]{1,0:T(8,128)S(1)}, u32[]{:S(2)}, u32[]{:S(2)}) %collective-permute-start.3) | collective-permute-done | bytes 327712 | tf_op jit(solution)/shard_map/ppermute | solution.py:168
  54.9 0.9 reshape.61
  55.8 13.6 %all-to-all-start = ((f32[64,2,640]{2,1,0:T(2,128)}), f32[64,2,640]{2,1,0:T(2,128)S(1)}, u32[]{:S(2)}, u32[]{:S(2)}) async-start(f32[64,2,640]{2,1,0:T(2,128)} %reshape.61), calls=%async_computation | async-start | bytes 655360 | tf_op jit(solution)/shard_map/all_to_all | solution.py:172
  69.4 5.7 %all-gather.2.cloned.1.call-done = bf16[1152,1536]{0,1:T(8,128)(2,1)} async-done(((bf16[1152,192]{0,1:T(8,128)(2,1)}), bf16[1152,1536]{0,1:T(8,128)(2,1)}) %all-gather.2.cloned.1.call-update) | async-done | bytes 3538960 | tf_op jit(solution)/shard_map/all_gather | solution.py:160
  75.1 2.9 %far_sums.1 = (f32[1024,128]{1,0:T(8,128)S(1)}, f32[1024,128]{1,0:T(8,128)S(1)}) custom-call(s32[1]{0:T(128)} %bitcast.y_ref, bf16[256,1152]{1,0:T(8,128)(2,1)S(1)} %get-tuple-element.13.rows_ref, bf16[1536,1152]{1,0:T(8,128)(2,1)} %bitcast.35), custom_call_target="tpu_custom_call" | custom-call | flops 603979776 | bytes 3850240 | tf_op jit(solution)/shard_map/far_sums/pallas_call | solution.py:110
  78.1 1.9 %collective-permute-start.2 = (f32[1024,128]{1,0:T(8,128)S(1)}, f32[1024,128]{1,0:T(8,128)S(1)}, u32[]{:S(2)}, u32[]{:S(2)}) collective-permute-start(f32[1024,128]{1,0:T(8,128)S(1)} %get-tuple-element.15), channel_id=1, source_target_pairs={{0,1},{1,0},{2,3},{3,2},{4,5},{5,4},{6,7},{7,6},{8,9},{9,8},{10,11... | collective-permute-start | bytes 1572872 | tf_op jit(solution)/shard_map/ppermute | solution.py:168
  80.0 5.2 %all-to-all-done = f32[64,2,640]{2,1,0:T(2,128)S(1)} async-done(((f32[64,2,640]{2,1,0:T(2,128)}), f32[64,2,640]{2,1,0:T(2,128)S(1)}, u32[]{:S(2)}, u32[]{:S(2)}) %all-to-all-start) | async-done | bytes 327712 | tf_op jit(solution)/shard_map/all_to_all | solution.py:172
  85.2 0.1 reduce_sum.27
  85.3 0.1 slice_bitcast_fusion.2
  85.4 0.1 reshape.63
  85.5 0.0 collective-permute-done.2
  85.5 0.0 copy-start.4
  85.5 0.9 add.32
  86.4 0.0 copy-start.2
  86.4 10.5 %all-to-all-start.1 = ((f32[64,16,128]{2,1,0:T(8,128)}), f32[64,16,128]{2,1,0:T(8,128)S(1)}, u32[]{:S(2)}, u32[]{:S(2)}) async-start(f32[64,16,128]{2,1,0:T(8,128)} %bitcast.7), calls=%async_computation.1 | async-start | bytes 1048576 | tf_op jit(solution)/shard_map/all_to_all | solution.py:172
  96.9 0.0 copy-done.4
  97.0 0.1 iota_compare_fusion
  97.0 19.4 %all-to-all-done.1 = f32[64,16,128]{2,1,0:T(8,128)S(1)} async-done(((f32[64,16,128]{2,1,0:T(8,128)}), f32[64,16,128]{2,1,0:T(8,128)S(1)}, u32[]{:S(2)}, u32[]{:S(2)}) %all-to-all-start.1) | async-done | bytes 524320 | tf_op jit(solution)/shard_map/all_to_all | solution.py:172
  116.5 0.1 pad_maximum_fusion
  116.6 0.1 reshape.65
  116.7 0.1 fusion.7
  116.8 0.1 reshape.66
  117.0 0.1 fusion.8
  117.1 0.0 copy-done.2
  117.1 0.5 select_reduce_fusion
  117.6 0.2 fusion.2
  117.9 1.6 %fusion.1 = bf16[1,2,48,256]{3,2,1,0:T(8,128)(2,1)S(1)} fusion(bf16[2,1024,256]{2,1,0:T(8,128)(2,1)} %param.10, f32[2,48,1024]{2,1,0:T(8,128)S(1)} %get-tuple-element.26, f32[2,48]{1,0:T(2,128)S(1)} %get-tuple-element.22, f32[2,48]{1,0:T(2,128)S(1)} %multiply_maximum_fusion, pred[2,1024]{1,0:T(4,128)(4,1)S(1)} %iota_compare_fusion, ...), kind=kOutput, calls=%fused_computation.3 | convolution fusion | flops 50798592 | bytes 1496192 | tf_op jit(solution)/shard_map/rhc,rcd->rhd/dot_general | solution.py:212
  119.4 0.7 copy.20
  (10 shorter events, 0.2 us)
Async XLA Ops:
  6.5 8.9 %copy-start = (bf16[1152,512]{1,0:T(8,128)(2,1)S(1)}, bf16[1152,512]{1,0:T(8,128)(2,1)}, u32[]{:S(2)}) copy-start(bf16[1152,512]{1,0:T(8,128)(2,1)} %param.8) | copy-start | bytes 3538948
  6.5 43.8 %copy-start.1 = (bf16[1152,192]{0,1:T(8,128)(2,1)S(1)}, bf16[1152,192]{0,1:T(8,128)(2,1)}, u32[]{:S(2)}) copy-start(bf16[1152,192]{0,1:T(8,128)(2,1)} %param.7) | copy-start | bytes 1327108
  6.5 9.2 %copy-start.3 = (bf16[32,1152]{1,0:T(8,128)(2,1)S(1)}, bf16[32,1152]{1,0:T(8,128)(2,1)}, u32[]{:S(2)}) copy-start(bf16[32,1152]{1,0:T(8,128)(2,1)} %param.6) | copy-start | bytes 221188
  6.5 68.6 %all-gather.2.cloned.1.call-start = ((), (), s32[]{:S(2)}) async-start(), calls=%async_computation.2 | async-start | bytes 3981312 | tf_op jit(solution)/shard_map/all_gather | solution.py:160
  7.3 43.1 %collective-permute-start = (bf16[1152,192]{0,1:T(8,128)(2,1)}, bf16[1152,192]{0,1:T(8,128)(2,1)S(1)}, u32[]{:S(2)}, u32[]{:S(2)}) collective-permute-start(bf16[1152,192]{0,1:T(8,128)(2,1)} %param.7), channel_id=1, source_target_pairs={{0,16},{16,32},{32,48},{48,64},{64,80},{80,96},{96,112},{112,0},{1... | collective-permute-start | bytes 1327112 | tf_op jit(solution)/shard_map/ppermute | solution.py:161
  10.9 39.5 %collective-permute-start.1 = (bf16[1152,192]{0,1:T(8,128)(2,1)}, bf16[1152,192]{0,1:T(8,128)(2,1)S(1)}, u32[]{:S(2)}, u32[]{:S(2)}) collective-permute-start(bf16[1152,192]{0,1:T(8,128)(2,1)} %param.7), channel_id=1, source_target_pairs={{0,112},{16,0},{32,16},{48,32},{64,48},{80,64},{96,80},{112,96},{1... | collective-permute-start | bytes 1327112 | tf_op jit(solution)/shard_map/ppermute | solution.py:162
  51.3 3.5 %collective-permute-start.3 = (f32[128,640]{1,0:T(8,128)S(1)}, f32[128,640]{1,0:T(8,128)S(1)}, u32[]{:S(2)}, u32[]{:S(2)}) collective-permute-start(f32[128,640]{1,0:T(8,128)S(1)} %get-tuple-element.17), channel_id=1, source_target_pairs={{0,1},{1,0},{2,3},{3,2},{4,5},{5,4},{6,7},{7,6},{8,9},{9,8},{10,11... | collective-permute-start | bytes 983048 | tf_op jit(solution)/shard_map/ppermute | solution.py:168
  55.8 29.4 %all-to-all-start = ((f32[64,2,640]{2,1,0:T(2,128)}), f32[64,2,640]{2,1,0:T(2,128)S(1)}, u32[]{:S(2)}, u32[]{:S(2)}) async-start(f32[64,2,640]{2,1,0:T(2,128)} %reshape.61), calls=%async_computation | async-start | bytes 655360 | tf_op jit(solution)/shard_map/all_to_all | solution.py:172
  78.1 7.4 %collective-permute-start.2 = (f32[1024,128]{1,0:T(8,128)S(1)}, f32[1024,128]{1,0:T(8,128)S(1)}, u32[]{:S(2)}, u32[]{:S(2)}) collective-permute-start(f32[1024,128]{1,0:T(8,128)S(1)} %get-tuple-element.15), channel_id=1, source_target_pairs={{0,1},{1,0},{2,3},{3,2},{4,5},{5,4},{6,7},{7,6},{8,9},{9,8},{10,11... | collective-permute-start | bytes 1572872 | tf_op jit(solution)/shard_map/ppermute | solution.py:168
  85.5 11.4 %copy-start.4 = (s32[2]{0:T(128)S(1)}, s32[2]{0:T(128)}, u32[]{:S(2)}) copy-start(s32[2]{0:T(128)} %param.11) | copy-start | bytes 28
  86.4 30.7 %copy-start.2 = (bf16[2,1024,256]{2,1,0:T(8,128)(2,1)S(1)}, bf16[2,1024,256]{2,1,0:T(8,128)(2,1)}, u32[]{:S(2)}) copy-start(bf16[2,1024,256]{2,1,0:T(8,128)(2,1)} %param.9) | copy-start | bytes 3145732
  86.4 30.0 %all-to-all-start.1 = ((f32[64,16,128]{2,1,0:T(8,128)}), f32[64,16,128]{2,1,0:T(8,128)S(1)}, u32[]{:S(2)}, u32[]{:S(2)}) async-start(f32[64,16,128]{2,1,0:T(8,128)} %bitcast.7), calls=%async_computation.1 | async-start | bytes 1048576 | tf_op jit(solution)/shard_map/all_to_all | solution.py:172
Sparse Core Ops, SparseCore 0:
  10.0 65.0 all-gather.1

commit v3 on v2

--- a/solution.py
+++ b/solution.py
@@ -86,19 +86,14 @@
         copies[-1].start()
     rest = held.shape[0] - FAR * columns
     held[FAR * columns :, :] = jnp.zeros((rest, held.shape[1]), held.dtype)
-    waited, done = 0, 0
-    while done < blocks:
-        last = min(done + 3, blocks)
-        while waited < FAR and waited * columns < last * LANES:
-            copies[waited].wait()
-            waited += 1
-        sums = times(rows_ref[...], held[done * LANES : last * LANES, :])
-        for block in range(done, last):
-            lanes = slice((block - done) * LANES, (block - done + 1) * LANES)
-            place = pl.ds(block, half, stride=blocks)
-            other_ref[place, :] = sums[:half, lanes]
-            same_ref[place, :] = sums[half:, lanes]
-        done = last
+    for copy in copies:
+        copy.wait()
+    sums = times(rows_ref[...], held[...])
+    for block in range(blocks):
+        lanes = slice(block * LANES, (block + 1) * LANES)
+        place = pl.ds(block, half, stride=blocks)
+        other_ref[place, :] = sums[:half, lanes]
+        same_ref[place, :] = sums[half:, lanes]
 
 
 def far_sums(y_index, rows, weights):
@@ -130,6 +125,48 @@
     )(y_index.reshape(1), rows, weights)
 
 
+def attend_body(lengths_ref, queries_ref, pairs_ref, keys_ref, values_ref, out_ref):
+    own_rows, _, head_size = queries_ref.shape
+    scale_factor = 1.0 / math.sqrt(head_size)
+    shares = []
+    for row in range(own_rows):
+        queries = queries_ref[row]
+        scores = times(queries, keys_ref[row]) * scale_factor
+        new_key = pairs_ref[row : row + 1, :head_size].astype(jnp.float32)
+        own_score = jnp.sum(queries.astype(jnp.float32) * new_key, axis=1, keepdims=True)
+        own_score = own_score * scale_factor
+        live_mask = lax.broadcasted_iota(jnp.int32, scores.shape, 1) < lengths_ref[row]
+        peak_score = jnp.max(jnp.where(live_mask, scores, -jnp.inf), axis=1, keepdims=True)
+        peak_score = jnp.maximum(peak_score, own_score)
+        raw_weights = jnp.where(live_mask, jnp.exp(scores - peak_score), 0.0)
+        own_raw = jnp.exp(own_score - peak_score)
+        totals = jnp.sum(raw_weights, axis=1, keepdims=True) + own_raw
+        weights = (raw_weights / totals).astype(jnp.bfloat16)
+        shares.append((weights, (own_raw / totals).astype(jnp.bfloat16)))
+    for row, (weights, own_weight) in enumerate(shares):
+        new_value = pairs_ref[row : row + 1, head_size:].astype(jnp.float32)
+        blended = jnp.dot(weights, values_ref[row], preferred_element_type=jnp.float32)
+        blended = blended + own_weight.astype(jnp.float32) * new_value
+        out_ref[row] = blended.astype(out_ref.dtype)
+
+
+def attend(lengths, queries, new_pairs, key_cache, value_cache):
+    in_vmem = pl.BlockSpec(memory_space=pltpu.VMEM)
+    return pl.pallas_call(
+        attend_body,
+        in_specs=[pl.BlockSpec(memory_space=pltpu.SMEM)] + [in_vmem] * 4,
+        out_specs=in_vmem,
+        out_shape=jax.ShapeDtypeStruct(queries.shape, queries.dtype),
+        compiler_params=pltpu.CompilerParams(vmem_limit_bytes=8 * 2**20),
+        cost_estimate=pl.CostEstimate(
+            flops=4 * queries.shape[1] * key_cache.size,
+            bytes_accessed=4 * key_cache.size,
+            transcendentals=queries.shape[0] * queries.shape[1] * key_cache.shape[1],
+        ),
+        name="attend",
+    )(lengths, queries, new_pairs, key_cache, value_cache)
+
+
 def shift_y(step):
     return [
         (SIDE * x + y, SIDE * x + (y + step) % SIDE) for x in range(SIDE) for y in range(SIDE)
@@ -143,7 +180,6 @@
     width = tokens.shape[1]
     columns = q_weight.shape[1]
     head_size = key_cache.shape[2]
-    slot_count = key_cache.shape[1]
     x_index = lax.axis_index("mx") // SIDE
     y_index = lax.axis_index("mx") % SIDE
     core = lax.axis_index("my") % 2
@@ -190,31 +226,7 @@
     query_rows = lax.dynamic_slice_in_dim(query_rows, (SIDE + 1 - y_index) % SIDE, SIDE, 2)
     queries = query_rows.reshape(own_rows, -1, head_size)
 
-    new_key = new_pairs[:, :head_size]
-    new_value = new_pairs[:, head_size:]
-    scale_factor = 1.0 / math.sqrt(head_size)
-    scores = (
-        jnp.einsum("rhd,rcd->rhc", queries, key_cache, preferred_element_type=jnp.float32)
-        * scale_factor
-    )
-    own_score = (
-        jnp.einsum("rhd,rd->rh", queries, new_key, preferred_element_type=jnp.float32)
-        * scale_factor
-    )
-    slot_index = lax.broadcasted_iota(jnp.int32, (1, 1, slot_count), 2)
-    live_mask = slot_index < lengths[:, None, None]
-    peak_score = jnp.maximum(jnp.max(jnp.where(live_mask, scores, -jnp.inf), axis=2), own_score)
-    raw_weights = jnp.where(live_mask, jnp.exp(scores - peak_score[:, :, None]), 0.0)
-    own_raw = jnp.exp(own_score - peak_score)
-    totals = jnp.sum(raw_weights, axis=2) + own_raw
-    weights = (raw_weights / totals[:, :, None]).astype(jnp.bfloat16)
-    own_weight = (own_raw / totals).astype(jnp.bfloat16)
-    blended = jnp.einsum("rhc,rcd->rhd", weights, value_cache, preferred_element_type=jnp.float32)
-    blended = (
-        blended
-        + own_weight.astype(jnp.float32)[:, :, None] * new_value.astype(jnp.float32)[:, None, :]
-    )
-    return blended.astype(jnp.bfloat16).reshape(own_rows, -1)
+    return attend(lengths, queries, new_pairs, key_cache, value_cache).reshape(own_rows, -1)
 
 
 def solution(mesh):

time: 127 us -> 127 us (level)
  matrix products: 2.22 us -> 0 us
    dot_general x3 -> x0, matrix products: 2.22 us -> none  [the longest x1 1.58 us: local(): jnp.einsum('rhc,rcd->rhd', weights, value_cache, preferred_element_type=j...]
    pallas_call x0 -> x1, Pallas kernels: none -> 1.4 us  [attend(): pl.pallas_call(attend_body, in_specs=[pl.BlockSpec(memory_space=pltpu.SME...]
where the time goes in v3:
time: 127 us
  starting transfers between devices  35.9 us (28%)
  blocking collectives  34.6 us (27%)
  waiting for transfers between devices  33 us (26%)
  between operations  13.6 us (11%)
  Pallas kernels  4.82 us (4%)
  local copies, waits for them, and re-layouts  2.39 us (2%)
  other arithmetic  2.24 us (2%)
    all_gather x1, blocking collectives, local(): lax.all_gather(tokens, 'mx', axis=0, tiled=True, axis_index_groups=x_rings)  34.6 us
    all_to_all x2, waiting for transfers between devices, exchange(): lax.all_to_all(sums, ('mx', 'my'), split_axis=0, concat_axis=0, axis_inde...  25 us
    all_to_all x2, starting transfers between devices, exchange(): lax.all_to_all(sums, ('mx', 'my'), split_axis=0, concat_axis=0, axis_inde...  23.9 us
    all_gather x1, waiting for transfers between devices, local(): lax.all_gather(q_weight, 'mx', axis=1, tiled=True, axis_index_groups=y_ri...  5.71 us
    ppermute x1, starting transfers between devices, local(): above = lax.ppermute(q_weight, 'mx', shift_y(-1))  4.49 us
    ppermute x2, starting transfers between devices, chip_sums(): swapped = lax.ppermute(other_sums, 'my', core_pairs)  3.84 us
    ppermute x1, starting transfers between devices, local(): below = lax.ppermute(q_weight, 'mx', shift_y(1))  3.6 us
  transfers between devices with their start and end apart: 7, of which 4 were waited for; matrix products, arithmetic and copies ran while one was open for 1% of the time, Pallas kernels for 3%

profile of v3, /device:TPU:2, one launch (start us, length us, event | category | flops | bytes accessed | tf_op | source)
XLA Modules:
  0.0 126.6 jit_solution(530636279238991209)
XLA Ops:
  6.5 0.0 copy-start
  6.5 0.0 copy-start.1
  6.5 0.0 copy-start.5
  6.5 0.0 all-gather.2.cloned.1.call-start
  6.5 0.7 all-gather.2.cloned.1.call-update
  7.3 3.6 %collective-permute-start = (bf16[1152,192]{0,1:T(8,128)(2,1)}, bf16[1152,192]{0,1:T(8,128)(2,1)S(1)}, u32[]{:S(2)}, u32[]{:S(2)}) collective-permute-start(bf16[1152,192]{0,1:T(8,128)(2,1)} %param.7), channel_id=1, source_target_pairs={{0,16},{16,32},{32,48},{48,64},{64,80},{80,96},{96,112},{112,0},{1... | collective-permute-start | bytes 1327112 | tf_op jit(solution)/shard_map/ppermute | solution.py:197
  10.9 4.5 %collective-permute-start.1 = (bf16[1152,192]{0,1:T(8,128)(2,1)}, bf16[1152,192]{0,1:T(8,128)(2,1)S(1)}, u32[]{:S(2)}, u32[]{:S(2)}) collective-permute-start(bf16[1152,192]{0,1:T(8,128)(2,1)} %param.7), channel_id=1, source_target_pairs={{0,112},{16,0},{32,16},{48,32},{64,48},{80,64},{96,80},{112,96},{1... | collective-permute-start | bytes 1327112 | tf_op jit(solution)/shard_map/ppermute | solution.py:198
  15.4 0.0 copy-done
  15.4 0.1 constant_dynamic-slice_fusion
  15.6 0.2 copy.13
  15.7 0.0 copy-done.5
  15.8 34.6 %all_gather.6.gathered_ref = bf16[256,1152]{1,0:T(8,128)(2,1)S(1)} all-gather(bf16[32,1152]{1,0:T(8,128)(2,1)S(1)} %copy-done.5), channel_id=1, replica_groups={{0,128,256,384,512,640,768,896},{16,144,272,400,528,656,784,912},{32,16..., dimensions={0}, use_global_device_ids=true | all-gather | bytes 663552 | tf_op jit(solution)/shard_map/all_gather | solution.py:199
  50.4 0.0 collective-permute-done
  50.4 0.0 collective-permute-done.1
  50.4 0.0 copy-done.1
  50.4 0.9 near_sums.1
  51.3 1.9 %collective-permute-start.3 = (f32[128,640]{1,0:T(8,128)S(1)}, f32[128,640]{1,0:T(8,128)S(1)}, u32[]{:S(2)}, u32[]{:S(2)}) collective-permute-start(f32[128,640]{1,0:T(8,128)S(1)} %get-tuple-element.17), channel_id=1, source_target_pairs={{0,1},{1,0},{2,3},{3,2},{4,5},{5,4},{6,7},{7,6},{8,9},{9,8},{10,11... | collective-permute-start | bytes 983048 | tf_op jit(solution)/shard_map/ppermute | solution.py:204
  53.2 1.6 %collective-permute-done.3 = f32[128,640]{1,0:T(8,128)S(1)} collective-permute-done((f32[128,640]{1,0:T(8,128)S(1)}, f32[128,640]{1,0:T(8,128)S(1)}, u32[]{:S(2)}, u32[]{:S(2)}) %collective-permute-start.3) | collective-permute-done | bytes 327712 | tf_op jit(solution)/shard_map/ppermute | solution.py:204
  54.9 0.9 reshape.36
  55.8 13.6 %all-to-all-start = ((f32[64,2,640]{2,1,0:T(2,128)}), f32[64,2,640]{2,1,0:T(2,128)S(1)}, u32[]{:S(2)}, u32[]{:S(2)}) async-start(f32[64,2,640]{2,1,0:T(2,128)} %reshape.36), calls=%async_computation | async-start | bytes 655360 | tf_op jit(solution)/shard_map/all_to_all | solution.py:208
  69.4 5.7 %all-gather.2.cloned.1.call-done = bf16[1152,1536]{0,1:T(8,128)(2,1)} async-done(((bf16[1152,192]{0,1:T(8,128)(2,1)}), bf16[1152,1536]{0,1:T(8,128)(2,1)}) %all-gather.2.cloned.1.call-update) | async-done | bytes 3538960 | tf_op jit(solution)/shard_map/all_gather | solution.py:196
  75.1 2.5 %far_sums.1 = (f32[1024,128]{1,0:T(8,128)S(1)}, f32[1024,128]{1,0:T(8,128)S(1)}) custom-call(s32[1]{0:T(128)} %bitcast.y_ref, bf16[256,1152]{1,0:T(8,128)(2,1)S(1)} %get-tuple-element.13.rows_ref, bf16[1536,1152]{1,0:T(8,128)(2,1)} %bitcast.27), custom_call_target="tpu_custom_call" | custom-call | flops 603979776 | bytes 3850240 | tf_op jit(solution)/shard_map/far_sums/pallas_call | solution.py:105
  77.7 1.9 %collective-permute-start.2 = (f32[1024,128]{1,0:T(8,128)S(1)}, f32[1024,128]{1,0:T(8,128)S(1)}, u32[]{:S(2)}, u32[]{:S(2)}) collective-permute-start(f32[1024,128]{1,0:T(8,128)S(1)} %get-tuple-element.15), channel_id=1, source_target_pairs={{0,1},{1,0},{2,3},{3,2},{4,5},{5,4},{6,7},{7,6},{8,9},{9,8},{10,11... | collective-permute-start | bytes 1572872 | tf_op jit(solution)/shard_map/ppermute | solution.py:204
  79.6 5.6 %all-to-all-done = f32[64,2,640]{2,1,0:T(2,128)S(1)} async-done(((f32[64,2,640]{2,1,0:T(2,128)}), f32[64,2,640]{2,1,0:T(2,128)S(1)}, u32[]{:S(2)}, u32[]{:S(2)}) %all-to-all-start) | async-done | bytes 327712 | tf_op jit(solution)/shard_map/all_to_all | solution.py:208
  85.2 0.1 reduce_sum.18
  85.3 0.1 slice_bitcast_fusion.2
  85.4 0.1 reshape.38.pairs_ref
  85.5 0.0 collective-permute-done.2
  85.5 0.8 add.26
  86.4 0.0 copy-start.2
  86.4 0.0 copy-start.3
  86.4 0.0 copy-start.4
  86.4 10.3 %all-to-all-start.1 = ((f32[64,16,128]{2,1,0:T(8,128)}), f32[64,16,128]{2,1,0:T(8,128)}, u32[]{:S(2)}, u32[]{:S(2)}) async-start(f32[64,16,128]{2,1,0:T(8,128)} %bitcast.28), calls=%async_computation.1 | async-start | bytes 1048576 | tf_op jit(solution)/shard_map/all_to_all | solution.py:208
  96.7 19.4 %all-to-all-done.1 = f32[64,16,128]{2,1,0:T(8,128)} async-done(((f32[64,16,128]{2,1,0:T(8,128)}), f32[64,16,128]{2,1,0:T(8,128)}, u32[]{:S(2)}, u32[]{:S(2)}) %all-to-all-start.1) | async-done | bytes 524320 | tf_op jit(solution)/shard_map/all_to_all | solution.py:208
  116.1 1.1 reduce_sum.19
  117.2 0.1 pad_maximum_fusion
  117.3 0.1 reshape.40
  117.5 0.1 fusion
  117.6 0.1 reshape.41.queries_ref
  117.7 0.0 copy-done.2
  117.7 0.0 copy-done.3
  117.7 0.0 copy-done.4
  117.7 1.4 %attend.1 = bf16[2,48,256]{2,1,0:T(8,128)(2,1)S(1)} custom-call(s32[2]{0:T(128)S(1)} %copy-done.4, bf16[2,48,256]{2,1,0:T(8,128)(2,1)S(1)} %reshape.41.queries_ref, bf16[2,512]{1,0:T(2,128)(2,1)S(1)} %reshape.38.pairs_ref, bf16[2,1024,256]{2,1,0:T(8,128)(2,1)S(1)} %copy-done.2, bf16[2,1024,256]{2,1,0:T(8,128)(2,1)S(1)} %copy-done.3), custom_call_target="tpu_custom_call" | custom-call | flops 100663296 | bytes 2097152 | tf_op jit(solution)/shard_map/attend/pallas_call | solution.py:155
  119.1 0.7 copy.15
  (6 shorter events, 0.1 us)
Async XLA Ops:
  6.5 8.9 %copy-start = (bf16[1152,512]{1,0:T(8,128)(2,1)S(1)}, bf16[1152,512]{1,0:T(8,128)(2,1)}, u32[]{:S(2)}) copy-start(bf16[1152,512]{1,0:T(8,128)(2,1)} %param.8) | copy-start | bytes 3538948
  6.5 43.8 %copy-start.1 = (bf16[1152,192]{0,1:T(8,128)(2,1)S(1)}, bf16[1152,192]{0,1:T(8,128)(2,1)}, u32[]{:S(2)}) copy-start(bf16[1152,192]{0,1:T(8,128)(2,1)} %param.7) | copy-start | bytes 1327108
  6.5 9.2 %copy-start.5 = (bf16[32,1152]{1,0:T(8,128)(2,1)S(1)}, bf16[32,1152]{1,0:T(8,128)(2,1)}, u32[]{:S(2)}) copy-start(bf16[32,1152]{1,0:T(8,128)(2,1)} %param.6) | copy-start | bytes 221188
  6.5 68.6 %all-gather.2.cloned.1.call-start = ((), (), s32[]{:S(2)}) async-start(), calls=%async_computation.2 | async-start | bytes 3981312 | tf_op jit(solution)/shard_map/all_gather | solution.py:196
  7.3 43.1 %collective-permute-start = (bf16[1152,192]{0,1:T(8,128)(2,1)}, bf16[1152,192]{0,1:T(8,128)(2,1)S(1)}, u32[]{:S(2)}, u32[]{:S(2)}) collective-permute-start(bf16[1152,192]{0,1:T(8,128)(2,1)} %param.7), channel_id=1, source_target_pairs={{0,16},{16,32},{32,48},{48,64},{64,80},{80,96},{96,112},{112,0},{1... | collective-permute-start | bytes 1327112 | tf_op jit(solution)/shard_map/ppermute | solution.py:197
  10.9 39.5 %collective-permute-start.1 = (bf16[1152,192]{0,1:T(8,128)(2,1)}, bf16[1152,192]{0,1:T(8,128)(2,1)S(1)}, u32[]{:S(2)}, u32[]{:S(2)}) collective-permute-start(bf16[1152,192]{0,1:T(8,128)(2,1)} %param.7), channel_id=1, source_target_pairs={{0,112},{16,0},{32,16},{48,32},{64,48},{80,64},{96,80},{112,96},{1... | collective-permute-start | bytes 1327112 | tf_op jit(solution)/shard_map/ppermute | solution.py:198
  51.3 3.5 %collective-permute-start.3 = (f32[128,640]{1,0:T(8,128)S(1)}, f32[128,640]{1,0:T(8,128)S(1)}, u32[]{:S(2)}, u32[]{:S(2)}) collective-permute-start(f32[128,640]{1,0:T(8,128)S(1)} %get-tuple-element.17), channel_id=1, source_target_pairs={{0,1},{1,0},{2,3},{3,2},{4,5},{5,4},{6,7},{7,6},{8,9},{9,8},{10,11... | collective-permute-start | bytes 983048 | tf_op jit(solution)/shard_map/ppermute | solution.py:204
  55.8 29.4 %all-to-all-start = ((f32[64,2,640]{2,1,0:T(2,128)}), f32[64,2,640]{2,1,0:T(2,128)S(1)}, u32[]{:S(2)}, u32[]{:S(2)}) async-start(f32[64,2,640]{2,1,0:T(2,128)} %reshape.36), calls=%async_computation | async-start | bytes 655360 | tf_op jit(solution)/shard_map/all_to_all | solution.py:208
  77.7 7.9 %collective-permute-start.2 = (f32[1024,128]{1,0:T(8,128)S(1)}, f32[1024,128]{1,0:T(8,128)S(1)}, u32[]{:S(2)}, u32[]{:S(2)}) collective-permute-start(f32[1024,128]{1,0:T(8,128)S(1)} %get-tuple-element.15), channel_id=1, source_target_pairs={{0,1},{1,0},{2,3},{3,2},{4,5},{5,4},{6,7},{7,6},{8,9},{9,8},{10,11... | collective-permute-start | bytes 1572872 | tf_op jit(solution)/shard_map/ppermute | solution.py:204
  86.4 31.3 %copy-start.2 = (bf16[2,1024,256]{2,1,0:T(8,128)(2,1)S(1)}, bf16[2,1024,256]{2,1,0:T(8,128)(2,1)}, u32[]{:S(2)}) copy-start(bf16[2,1024,256]{2,1,0:T(8,128)(2,1)} %keys_ref.1) | copy-start | bytes 3145732
  86.4 31.3 %copy-start.3 = (bf16[2,1024,256]{2,1,0:T(8,128)(2,1)S(1)}, bf16[2,1024,256]{2,1,0:T(8,128)(2,1)}, u32[]{:S(2)}) copy-start(bf16[2,1024,256]{2,1,0:T(8,128)(2,1)} %values_ref.1) | copy-start | bytes 3145732
  86.4 31.3 %copy-start.4 = (s32[2]{0:T(128)S(1)}, s32[2]{0:T(128)}, u32[]{:S(2)}) copy-start(s32[2]{0:T(128)} %lengths_ref.1) | copy-start | bytes 28
  86.4 29.7 %all-to-all-start.1 = ((f32[64,16,128]{2,1,0:T(8,128)}), f32[64,16,128]{2,1,0:T(8,128)}, u32[]{:S(2)}, u32[]{:S(2)}) async-start(f32[64,16,128]{2,1,0:T(8,128)} %bitcast.28), calls=%async_computation.1 | async-start | bytes 1048576 | tf_op jit(solution)/shard_map/all_to_all | solution.py:208
Sparse Core Ops, SparseCore 0:
  10.0 65.0 all-gather.1

commit v4 on v3

--- a/solution.py
+++ b/solution.py
@@ -70,24 +70,14 @@
     )(core.reshape(1), gathered, *pieces)
 
 
-def far_body(blocks, y_ref, rows_ref, weights_ref, other_ref, same_ref, held, sems):
-    columns = weights_ref.shape[0] // SIDE
+def far_body(blocks, rows_ref, *refs):
+    *pieces, other_ref, same_ref, held = refs
     half = rows_ref.shape[0] // 2
-    copies = []
-    for at in range(FAR):
-        source = lax.rem(y_ref[0] + 2 + at, SIDE) * columns
-        copies.append(
-            pltpu.make_async_copy(
-                weights_ref.at[pl.ds(pl.multiple_of(source, columns), columns), :],
-                held.at[pl.ds(at * columns, columns), :],
-                sems.at[at],
-            )
-        )
-        copies[-1].start()
-    rest = held.shape[0] - FAR * columns
-    held[FAR * columns :, :] = jnp.zeros((rest, held.shape[1]), held.dtype)
-    for copy in copies:
-        copy.wait()
+    at = 0
+    for piece in pieces:
+        held[at : at + piece.shape[0], :] = piece[...]
+        at += piece.shape[0]
+    held[at:, :] = jnp.zeros((held.shape[0] - at, held.shape[1]), held.dtype)
     sums = times(rows_ref[...], held[...])
     for block in range(blocks):
         lanes = slice(block * LANES, (block + 1) * LANES)
@@ -96,33 +86,25 @@
         same_ref[place, :] = sums[half:, lanes]
 
 
-def far_sums(y_index, rows, weights):
+def far_sums(rows, *pieces):
     half, width = rows.shape[0] // 2, rows.shape[1]
-    columns = weights.shape[0] // SIDE
-    blocks = -(-FAR * columns // LANES)
+    blocks = -(-sum(piece.shape[0] for piece in pieces) // LANES)
     product = jax.ShapeDtypeStruct((half * blocks, LANES), jnp.float32)
     in_vmem = pl.BlockSpec(memory_space=pltpu.VMEM)
     return pl.pallas_call(
         functools.partial(far_body, blocks),
-        in_specs=[
-            pl.BlockSpec(memory_space=pltpu.SMEM),
-            in_vmem,
-            pl.BlockSpec(memory_space=pltpu.HBM),
-        ],
+        in_specs=[in_vmem] * (1 + len(pieces)),
         out_specs=[in_vmem, in_vmem],
         out_shape=[product, product],
-        scratch_shapes=[
-            pltpu.VMEM((blocks * LANES, width), jnp.bfloat16),
-            pltpu.SemaphoreType.DMA((FAR,)),
-        ],
-        compiler_params=pltpu.CompilerParams(vmem_limit_bytes=50 * 2**20),
+        scratch_shapes=[pltpu.VMEM((blocks * LANES, width), jnp.bfloat16)],
+        compiler_params=pltpu.CompilerParams(vmem_limit_bytes=20 * 2**20),
         cost_estimate=pl.CostEstimate(
             flops=4 * half * width * blocks * LANES,
-            bytes_accessed=2 * width * (2 * half + FAR * columns) + 8 * half * blocks * LANES,
+            bytes_accessed=2 * width * (2 * half + blocks * LANES) + 8 * half * blocks * LANES,
             transcendentals=0,
         ),
         name="far_sums",
-    )(y_index.reshape(1), rows, weights)
+    )(rows, *pieces)
 
 
 def attend_body(lengths_ref, queries_ref, pairs_ref, keys_ref, values_ref, out_ref):
@@ -185,7 +167,6 @@
     core = lax.axis_index("my") % 2
 
     x_rings = [[SIDE * x + y for x in range(SIDE)] for y in range(SIDE)]
-    y_rings = [[SIDE * x + y for y in range(SIDE)] for x in range(SIDE)]
     core_pairs = [(i, i ^ 1) for i in range(my_count)]
     plane_groups = [
         [(SIDE * x + y) * my_count + 2 * plane + one for plane in range(planes) for x in range(SIDE)]
@@ -193,10 +174,20 @@
         for one in range(2)
     ]
 
-    weights_here = lax.all_gather(q_weight, "mx", axis=1, tiled=True, axis_index_groups=y_rings)
-    below = lax.ppermute(q_weight, "mx", shift_y(1))
-    above = lax.ppermute(q_weight, "mx", shift_y(-1))
-    gathered = lax.all_gather(tokens, "mx", axis=0, tiled=True, axis_index_groups=x_rings)
+    below = [lax.ppermute(q_weight, "mx", shift_y(1))]
+    above = [lax.ppermute(q_weight, "mx", shift_y(-1))]
+    copies = jnp.broadcast_to(tokens, (SIDE, *tokens.shape))
+    gathered = lax.all_to_all(
+        copies, "mx", split_axis=0, concat_axis=0, axis_index_groups=x_rings
+    ).reshape(-1, width)
+    for _ in range(2):
+        below.append(lax.ppermute(below[-1], "mx", shift_y(1)))
+        above.append(lax.ppermute(above[-1], "mx", shift_y(-1)))
+    half = columns // 2
+    opposite = (
+        lax.ppermute(below[2][:, :half], "mx", shift_y(1)),
+        lax.ppermute(above[2][:, half:], "mx", shift_y(-1)),
+    )
     pair_columns = kv_weight.shape[1] // SIDE
     pair_weight = lax.dynamic_slice_in_dim(kv_weight, x_index * pair_columns, pair_columns, 1)
 
@@ -212,12 +203,13 @@
         return sums.astype(jnp.bfloat16).reshape(SIDE, own_rows, -1)
 
     rows, *near = near_sums(
-        planes, own_rows, core, gathered, below.T, q_weight.T, above.T, pair_weight.T
+        planes, own_rows, core, gathered, below[0].T, q_weight.T, above[0].T, pair_weight.T
     )
     near = exchange(chip_sums(*near))
     new_pairs = near[:, :, NEAR * columns :].transpose(1, 0, 2).reshape(own_rows, -1)
     near = near[:, :, : NEAR * columns].transpose(1, 0, 2)
-    far = chip_sums(*far_sums(y_index, rows, weights_here.T))
+    pieces = above[1], above[2], *opposite, below[2], below[1]
+    far = chip_sums(*far_sums(rows, *(piece.T for piece in pieces)))
     far, near, new_pairs = lax.optimization_barrier((far, near, new_pairs))
     far = exchange(far)
     far = far[:, :, : FAR * columns].transpose(1, 0, 2)

time: 127 us -> 131 us (1.031)
  the two profiles are of different devices: /device:TPU:2 before, /device:TPU:48 now
where the time goes in v4:
time: 131 us; the launch traced here: 130 us
  starting transfers between devices  73.4 us (56%)
  waiting for transfers between devices  43.5 us (33%)
  Pallas kernels  6.14 us (5%)
  local copies, waits for them, and re-layouts  4.31 us (3%)
  other arithmetic  2.26 us (2%)
    all_to_all x2, starting transfers between devices, exchange(): lax.all_to_all(sums, ('mx', 'my'), split_axis=0, concat_axis=0, axis_inde...  35.4 us
    all_to_all x2, waiting for transfers between devices, exchange(): lax.all_to_all(sums, ('mx', 'my'), split_axis=0, concat_axis=0, axis_inde...  19.7 us
    ppermute x1, waiting for transfers between devices, local(): above = [lax.ppermute(q_weight, 'mx', shift_y(-1))]  7.64 us
    ppermute x2, starting transfers between devices, local(): below.append(lax.ppermute(below[-1], 'mx', shift_y(1)))  7.52 us
    ppermute x2, waiting for transfers between devices, local(): below.append(lax.ppermute(below[-1], 'mx', shift_y(1)))  7.26 us
    all_to_all x1, starting transfers between devices, local(): lax.all_to_all(copies, 'mx', split_axis=0, concat_axis=0, axis_index_grou...  6.76 us
    ppermute x2, starting transfers between devices, local(): above.append(lax.ppermute(above[-1], 'mx', shift_y(-1)))  5.82 us
    ppermute x1, waiting for transfers between devices, local(): lax.ppermute(above[2][:, half:], 'mx', shift_y(-1))  5.64 us
  transfers between devices with their start and end apart: 13, of which 6 were waited for; matrix products, arithmetic and copies ran while one was open for 1% of the time, Pallas kernels for 4%

profile of v4, /device:TPU:48, one launch (start us, length us, event | category | flops | bytes accessed | tf_op | source)
XLA Modules:
  0.0 130.0 jit_solution(14894797252766824541)
XLA Ops:
  0.0 0.0 copy-start
  0.0 1.9 %broadcast_in_dim.3 = bf16[8,32,1152]{2,1,0:T(8,128)(2,1)} broadcast(bf16[32,1152]{1,0:T(8,128)(2,1)} %param.6), dimensions={1,2} | broadcast | bytes 663552 | tf_op jit(solution)/shard_map/broadcast_in_dim | solution.py:179
  1.9 6.8 %all-to-all-start = ((bf16[8,32,1152]{2,1,0:T(8,128)(2,1)}), bf16[8,32,1152]{2,1,0:T(8,128)(2,1)S(1)}, u32[]{:S(2)}, u32[]{:S(2)}) async-start(bf16[8,32,1152]{2,1,0:T(8,128)(2,1)} %broadcast_in_dim.3), calls=%async_computation | async-start | bytes 1179648 | tf_op jit(solution)/shard_map/all_to_all | solution.py:180
  8.6 0.0 copy-done.3
  8.6 2.2 %collective-permute-start.1 = (bf16[1152,192]{0,1:T(8,128)(2,1)S(1)}, bf16[1152,192]{0,1:T(8,128)(2,1)S(1)}, u32[]{:S(2)}, u32[]{:S(2)}) collective-permute-start(bf16[1152,192]{0,1:T(8,128)(2,1)S(1)} %copy-done.3), channel_id=1, source_target_pairs={{0,112},{16,0},{32,16},{48,32},{64,48},{80,64},{96,80},{112,96},{1... | collective-permute-start | bytes 1327112 | tf_op jit(solution)/shard_map/ppermute | solution.py:178
  10.9 4.8 %collective-permute-start = (bf16[1152,192]{0,1:T(8,128)(2,1)S(1)}, bf16[1152,192]{0,1:T(8,128)(2,1)}, u32[]{:S(2)}, u32[]{:S(2)}) collective-permute-start(bf16[1152,192]{0,1:T(8,128)(2,1)S(1)} %copy-done.3), channel_id=1, source_target_pairs={{0,16},{16,32},{32,48},{48,64},{64,80},{80,96},{96,112},{112,0},{1... | collective-permute-start | bytes 1327112 | tf_op jit(solution)/shard_map/ppermute | solution.py:177
  15.7 7.6 %collective-permute-done.1 = bf16[1152,192]{0,1:T(8,128)(2,1)S(1)} collective-permute-done((bf16[1152,192]{0,1:T(8,128)(2,1)S(1)}, bf16[1152,192]{0,1:T(8,128)(2,1)S(1)}, u32[]{:S(2)}, u32[]{:S(2)}) %collective-permute-start.1) | collective-permute-done | bytes 442400 | tf_op jit(solution)/shard_map/ppermute | solution.py:178
  23.4 1.9 %collective-permute-start.2 = (bf16[1152,192]{0,1:T(8,128)(2,1)S(1)}, bf16[1152,192]{0,1:T(8,128)(2,1)}, u32[]{:S(2)}, u32[]{:S(2)}) collective-permute-start(bf16[1152,192]{0,1:T(8,128)(2,1)S(1)} %collective-permute-done.1), channel_id=1, source_target_pairs={{0,112},{16,0},{32,16},{48,32},{64,48},{80,64},{96,80},{112,96},{1... | collective-permute-start | bytes 1327112 | tf_op jit(solution)/shard_map/ppermute | solution.py:185
  25.3 0.0 collective-permute-done
  25.3 5.1 %collective-permute-start.4 = (bf16[1152,192]{0,1:T(8,128)(2,1)}, bf16[1152,192]{0,1:T(8,128)(2,1)}, u32[]{:S(2)}, u32[]{:S(2)}) collective-permute-start(bf16[1152,192]{0,1:T(8,128)(2,1)} %collective-permute-done), channel_id=1, source_target_pairs={{0,16},{16,32},{32,48},{48,64},{64,80},{80,96},{96,112},{112,0},{1... | collective-permute-start | bytes 1327112 | tf_op jit(solution)/shard_map/ppermute | solution.py:184
  30.4 0.0 copy-done
  30.5 0.1 constant_dynamic-slice_fusion
  30.6 0.2 copy.13
  30.8 0.0 all-to-all-done
  30.8 1.9 %near_sums.1 = (bf16[256,1152]{1,0:T(8,128)(2,1)S(1)}, f32[128,640]{1,0:T(8,128)S(1)}, f32[128,640]{1,0:T(8,128)S(1)}) custom-call(s32[1]{0:T(128)} %bitcast.core_ref, bf16[256,1152]{1,0:T(8,128)(2,1)S(1)} %bitcast.27, bf16[192,1152]{1,0:T(8,128)(2,1)} %bitcast.2.below_ref, bf16[192,1152]{1,0:T(8,128)(2,1)S(1)} %bitcast.31, bf16[192,1152]{1,0:T(8,128)(2,1)S(1)} %bitcast.32, ...), custom_call_target="tpu_custom_call" | custom-call | flops 528482304 | bytes 3309568 | tf_op jit(solution)/shard_map/near_sums/pallas_call | solution.py:57
  32.7 1.9 %collective-permute-start.9 = (f32[128,640]{1,0:T(8,128)S(1)}, f32[128,640]{1,0:T(8,128)S(1)}, u32[]{:S(2)}, u32[]{:S(2)}) collective-permute-start(f32[128,640]{1,0:T(8,128)S(1)} %get-tuple-element.17), channel_id=1, source_target_pairs={{0,1},{1,0},{2,3},{3,2},{4,5},{5,4},{6,7},{7,6},{8,9},{9,8},{10,11... | collective-permute-start | bytes 983048 | tf_op jit(solution)/shard_map/ppermute | solution.py:195
  34.6 7.3 %collective-permute-done.4 = bf16[1152,192]{0,1:T(8,128)(2,1)} collective-permute-done((bf16[1152,192]{0,1:T(8,128)(2,1)}, bf16[1152,192]{0,1:T(8,128)(2,1)}, u32[]{:S(2)}, u32[]{:S(2)}) %collective-permute-start.4) | collective-permute-done | bytes 442400 | tf_op jit(solution)/shard_map/ppermute | solution.py:184
  41.9 2.4 %collective-permute-start.5 = (bf16[1152,192]{0,1:T(8,128)(2,1)}, bf16[1152,192]{0,1:T(8,128)(2,1)S(1)}, u32[]{:S(2)}, u32[]{:S(2)}) collective-permute-start(bf16[1152,192]{0,1:T(8,128)(2,1)} %collective-permute-done.4), channel_id=1, source_target_pairs={{0,16},{16,32},{32,48},{48,64},{64,80},{80,96},{96,112},{112,0},{1... | collective-permute-start | bytes 1327112 | tf_op jit(solution)/shard_map/ppermute | solution.py:184
  44.3 0.0 collective-permute-done.2
  44.3 3.9 %collective-permute-start.3 = (bf16[1152,192]{0,1:T(8,128)(2,1)}, bf16[1152,192]{0,1:T(8,128)(2,1)S(1)}, u32[]{:S(2)}, u32[]{:S(2)}) collective-permute-start(bf16[1152,192]{0,1:T(8,128)(2,1)} %collective-permute-done.2), channel_id=1, source_target_pairs={{0,112},{16,0},{32,16},{48,32},{64,48},{80,64},{96,80},{112,96},{1... | collective-permute-start | bytes 1327112 | tf_op jit(solution)/shard_map/ppermute | solution.py:185
  48.2 0.0 collective-permute-done.9
  48.3 0.9 reshape.36
  49.2 22.3 %all-to-all-start.1 = ((f32[64,2,640]{2,1,0:T(2,128)}), f32[64,2,640]{2,1,0:T(2,128)S(1)}, u32[]{:S(2)}, u32[]{:S(2)}) async-start(f32[64,2,640]{2,1,0:T(2,128)} %reshape.36), calls=%async_computation.1 | async-start | bytes 655360 | tf_op jit(solution)/shard_map/all_to_all | solution.py:199
  71.5 0.0 collective-permute-done.5
  71.6 5.1 %collective-permute-start.6 = (bf16[1152,96]{0,1:T(8,128)(2,1)S(1)}, bf16[1152,96]{0,1:T(8,128)(2,1)S(1)}, u32[]{:S(2)}, u32[]{:S(2)}) collective-permute-start(bf16[1152,96]{0,1:T(8,128)(2,1)S(1)} %slice.20), channel_id=1, source_target_pairs={{0,16},{16,32},{32,48},{48,64},{64,80},{80,96},{96,112},{112,0},{1... | collective-permute-start | bytes 663560 | tf_op jit(solution)/shard_map/ppermute | solution.py:188
  76.7 0.0 collective-permute-done.3
  76.7 1.9 %collective-permute-start.7 = (bf16[1152,96]{0,1:T(8,128)(2,1)S(1)}, bf16[1152,96]{0,1:T(8,128)(2,1)S(1)}, u32[]{:S(2)}, u32[]{:S(2)}) collective-permute-start(bf16[1152,96]{0,1:T(8,128)(2,1)S(1)} %slice.21), channel_id=1, source_target_pairs={{0,112},{16,0},{32,16},{48,32},{64,48},{80,64},{96,80},{112,96},{1... | collective-permute-start | bytes 663560 | tf_op jit(solution)/shard_map/ppermute | solution.py:189
  78.7 1.5 %collective-permute-done.6 = bf16[1152,96]{0,1:T(8,128)(2,1)S(1)} collective-permute-done((bf16[1152,96]{0,1:T(8,128)(2,1)S(1)}, bf16[1152,96]{0,1:T(8,128)(2,1)S(1)}, u32[]{:S(2)}, u32[]{:S(2)}) %collective-permute-start.6) | collective-permute-done | bytes 221216 | tf_op jit(solution)/shard_map/ppermute | solution.py:188
  80.1 5.6 %collective-permute-done.7 = bf16[1152,96]{0,1:T(8,128)(2,1)S(1)} collective-permute-done((bf16[1152,96]{0,1:T(8,128)(2,1)S(1)}, bf16[1152,96]{0,1:T(8,128)(2,1)S(1)}, u32[]{:S(2)}, u32[]{:S(2)}) %collective-permute-start.7) | collective-permute-done | bytes 221216 | tf_op jit(solution)/shard_map/ppermute | solution.py:189
  85.8 2.8 %far_sums.1 = (f32[1024,128]{1,0:T(8,128)}, f32[1024,128]{1,0:T(8,128)S(1)}) custom-call(bf16[256,1152]{1,0:T(8,128)(2,1)S(1)} %get-tuple-element.13.rows_ref, bf16[192,1152]{1,0:T(8,128)(2,1)} %bitcast.6.refs_0_, bf16[192,1152]{1,0:T(8,128)(2,1)S(1)} %bitcast.29, bf16[96,1152]{1,0:T(8,128)(2,1)S(1)} %bitcast.33, bf16[96,1152]{1,0:T(8,128)(2,1)S(1)} %bitcast.34, ...), custom_call_target="tpu_custom_call" | custom-call | flops 603979776 | bytes 3997696 | tf_op jit(solution)/shard_map/far_sums/pallas_call | solution.py:94
  88.6 1.9 %collective-permute-start.8 = (f32[1024,128]{1,0:T(8,128)}, f32[1024,128]{1,0:T(8,128)S(1)}, u32[]{:S(2)}, u32[]{:S(2)}) collective-permute-start(f32[1024,128]{1,0:T(8,128)} %get-tuple-element.15), channel_id=1, source_target_pairs={{0,1},{1,0},{2,3},{3,2},{4,5},{5,4},{6,7},{7,6},{8,9},{9,8},{10,11... | collective-permute-start | bytes 1572872 | tf_op jit(solution)/shard_map/ppermute | solution.py:195
  90.5 0.0 all-to-all-done.1
  90.6 0.1 reduce_sum.18
  90.7 0.1 slice_bitcast_fusion.2
  90.8 0.1 reshape.38.pairs_ref
  90.9 1.8 %collective-permute-done.8 = f32[1024,128]{1,0:T(8,128)S(1)} collective-permute-done((f32[1024,128]{1,0:T(8,128)}, f32[1024,128]{1,0:T(8,128)S(1)}, u32[]{:S(2)}, u32[]{:S(2)}) %collective-permute-start.8) | collective-permute-done | bytes 524320 | tf_op jit(solution)/shard_map/ppermute | solution.py:195
  92.6 0.9 add.25
  93.5 13.1 %all-to-all-start.2 = ((f32[64,16,128]{2,1,0:T(8,128)}), f32[64,16,128]{2,1,0:T(8,128)}, u32[]{:S(2)}, u32[]{:S(2)}) async-start(f32[64,16,128]{2,1,0:T(8,128)} %bitcast.36), calls=%async_computation.2 | async-start | bytes 1048576 | tf_op jit(solution)/shard_map/all_to_all | solution.py:199
  106.6 19.7 %all-to-all-done.2 = f32[64,16,128]{2,1,0:T(8,128)} async-done(((f32[64,16,128]{2,1,0:T(8,128)}), f32[64,16,128]{2,1,0:T(8,128)}, u32[]{:S(2)}, u32[]{:S(2)}) %all-to-all-start.2) | async-done | bytes 524320 | tf_op jit(solution)/shard_map/all_to_all | solution.py:199
  126.3 1.1 reduce_sum.19
  127.4 0.1 pad_maximum_fusion
  127.6 0.1 reshape.40
  127.7 0.1 fusion
  127.8 0.1 reshape.41.queries_ref
  127.9 0.0 copy-done.1
  127.9 0.0 copy-done.2
  127.9 1.4 %attend.1 = bf16[2,48,256]{2,1,0:T(8,128)(2,1)S(1)} custom-call(s32[2]{0:T(128)S(1)} %copy-done.4, bf16[2,48,256]{2,1,0:T(8,128)(2,1)S(1)} %reshape.41.queries_ref, bf16[2,512]{1,0:T(2,128)(2,1)S(1)} %reshape.38.pairs_ref, bf16[2,1024,256]{2,1,0:T(8,128)(2,1)S(1)} %copy-done.1, bf16[2,1024,256]{2,1,0:T(8,128)(2,1)S(1)} %copy-done.2), custom_call_target="tpu_custom_call" | custom-call | flops 100663296 | bytes 2097152 | tf_op jit(solution)/shard_map/attend/pallas_call | solution.py:137
  129.3 0.7 copy.15
  (13 shorter events, 0.2 us)
Async XLA Ops:
  0.0 30.4 %copy-start = (bf16[1152,512]{1,0:T(8,128)(2,1)S(1)}, bf16[1152,512]{1,0:T(8,128)(2,1)}, u32[]{:S(2)}) copy-start(bf16[1152,512]{1,0:T(8,128)(2,1)} %param.8) | copy-start | bytes 3538948
  0.0 8.6 %copy-start.3 = (bf16[1152,192]{0,1:T(8,128)(2,1)S(1)}, bf16[1152,192]{0,1:T(8,128)(2,1)}, u32[]{:S(2)}) copy-start(bf16[1152,192]{0,1:T(8,128)(2,1)} %param.7) | copy-start | bytes 1327108
  1.9 28.9 %all-to-all-start = ((bf16[8,32,1152]{2,1,0:T(8,128)(2,1)}), bf16[8,32,1152]{2,1,0:T(8,128)(2,1)S(1)}, u32[]{:S(2)}, u32[]{:S(2)}) async-start(bf16[8,32,1152]{2,1,0:T(8,128)(2,1)} %broadcast_in_dim.3), calls=%async_computation | async-start | bytes 1179648 | tf_op jit(solution)/shard_map/all_to_all | solution.py:180
  8.6 14.7 %collective-permute-start.1 = (bf16[1152,192]{0,1:T(8,128)(2,1)S(1)}, bf16[1152,192]{0,1:T(8,128)(2,1)S(1)}, u32[]{:S(2)}, u32[]{:S(2)}) collective-permute-start(bf16[1152,192]{0,1:T(8,128)(2,1)S(1)} %copy-done.3), channel_id=1, source_target_pairs={{0,112},{16,0},{32,16},{48,32},{64,48},{80,64},{96,80},{112,96},{1... | collective-permute-start | bytes 1327112 | tf_op jit(solution)/shard_map/ppermute | solution.py:178
  10.9 14.4 %collective-permute-start = (bf16[1152,192]{0,1:T(8,128)(2,1)S(1)}, bf16[1152,192]{0,1:T(8,128)(2,1)}, u32[]{:S(2)}, u32[]{:S(2)}) collective-permute-start(bf16[1152,192]{0,1:T(8,128)(2,1)S(1)} %copy-done.3), channel_id=1, source_target_pairs={{0,16},{16,32},{32,48},{48,64},{64,80},{80,96},{96,112},{112,0},{1... | collective-permute-start | bytes 1327112 | tf_op jit(solution)/shard_map/ppermute | solution.py:177
  23.4 20.9 %collective-permute-start.2 = (bf16[1152,192]{0,1:T(8,128)(2,1)S(1)}, bf16[1152,192]{0,1:T(8,128)(2,1)}, u32[]{:S(2)}, u32[]{:S(2)}) collective-permute-start(bf16[1152,192]{0,1:T(8,128)(2,1)S(1)} %collective-permute-done.1), channel_id=1, source_target_pairs={{0,112},{16,0},{32,16},{48,32},{64,48},{80,64},{96,80},{112,96},{1... | collective-permute-start | bytes 1327112 | tf_op jit(solution)/shard_map/ppermute | solution.py:185
  25.3 16.6 %collective-permute-start.4 = (bf16[1152,192]{0,1:T(8,128)(2,1)}, bf16[1152,192]{0,1:T(8,128)(2,1)}, u32[]{:S(2)}, u32[]{:S(2)}) collective-permute-start(bf16[1152,192]{0,1:T(8,128)(2,1)} %collective-permute-done), channel_id=1, source_target_pairs={{0,16},{16,32},{32,48},{48,64},{64,80},{80,96},{96,112},{112,0},{1... | collective-permute-start | bytes 1327112 | tf_op jit(solution)/shard_map/ppermute | solution.py:184
  32.7 15.5 %collective-permute-start.9 = (f32[128,640]{1,0:T(8,128)S(1)}, f32[128,640]{1,0:T(8,128)S(1)}, u32[]{:S(2)}, u32[]{:S(2)}) collective-permute-start(f32[128,640]{1,0:T(8,128)S(1)} %get-tuple-element.17), channel_id=1, source_target_pairs={{0,1},{1,0},{2,3},{3,2},{4,5},{5,4},{6,7},{7,6},{8,9},{9,8},{10,11... | collective-permute-start | bytes 983048 | tf_op jit(solution)/shard_map/ppermute | solution.py:195
  41.9 29.6 %collective-permute-start.5 = (bf16[1152,192]{0,1:T(8,128)(2,1)}, bf16[1152,192]{0,1:T(8,128)(2,1)S(1)}, u32[]{:S(2)}, u32[]{:S(2)}) collective-permute-start(bf16[1152,192]{0,1:T(8,128)(2,1)} %collective-permute-done.4), channel_id=1, source_target_pairs={{0,16},{16,32},{32,48},{48,64},{64,80},{80,96},{96,112},{112,0},{1... | collective-permute-start | bytes 1327112 | tf_op jit(solution)/shard_map/ppermute | solution.py:184
  44.3 32.4 %collective-permute-start.3 = (bf16[1152,192]{0,1:T(8,128)(2,1)}, bf16[1152,192]{0,1:T(8,128)(2,1)S(1)}, u32[]{:S(2)}, u32[]{:S(2)}) collective-permute-start(bf16[1152,192]{0,1:T(8,128)(2,1)} %collective-permute-done.2), channel_id=1, source_target_pairs={{0,112},{16,0},{32,16},{48,32},{64,48},{80,64},{96,80},{112,96},{1... | collective-permute-start | bytes 1327112 | tf_op jit(solution)/shard_map/ppermute | solution.py:185
  49.2 41.3 %all-to-all-start.1 = ((f32[64,2,640]{2,1,0:T(2,128)}), f32[64,2,640]{2,1,0:T(2,128)S(1)}, u32[]{:S(2)}, u32[]{:S(2)}) async-start(f32[64,2,640]{2,1,0:T(2,128)} %reshape.36), calls=%async_computation.1 | async-start | bytes 655360 | tf_op jit(solution)/shard_map/all_to_all | solution.py:199
  71.6 8.6 %collective-permute-start.6 = (bf16[1152,96]{0,1:T(8,128)(2,1)S(1)}, bf16[1152,96]{0,1:T(8,128)(2,1)S(1)}, u32[]{:S(2)}, u32[]{:S(2)}) collective-permute-start(bf16[1152,96]{0,1:T(8,128)(2,1)S(1)} %slice.20), channel_id=1, source_target_pairs={{0,16},{16,32},{32,48},{48,64},{64,80},{80,96},{96,112},{112,0},{1... | collective-permute-start | bytes 663560 | tf_op jit(solution)/shard_map/ppermute | solution.py:188
  76.7 9.0 %collective-permute-start.7 = (bf16[1152,96]{0,1:T(8,128)(2,1)S(1)}, bf16[1152,96]{0,1:T(8,128)(2,1)S(1)}, u32[]{:S(2)}, u32[]{:S(2)}) collective-permute-start(bf16[1152,96]{0,1:T(8,128)(2,1)S(1)} %slice.21), channel_id=1, source_target_pairs={{0,112},{16,0},{32,16},{48,32},{64,48},{80,64},{96,80},{112,96},{1... | collective-permute-start | bytes 663560 | tf_op jit(solution)/shard_map/ppermute | solution.py:189
  88.6 4.0 %collective-permute-start.8 = (f32[1024,128]{1,0:T(8,128)}, f32[1024,128]{1,0:T(8,128)S(1)}, u32[]{:S(2)}, u32[]{:S(2)}) collective-permute-start(f32[1024,128]{1,0:T(8,128)} %get-tuple-element.15), channel_id=1, source_target_pairs={{0,1},{1,0},{2,3},{3,2},{4,5},{5,4},{6,7},{7,6},{8,9},{9,8},{10,11... | collective-permute-start | bytes 1572872 | tf_op jit(solution)/shard_map/ppermute | solution.py:195
  93.5 34.4 %copy-start.1 = (bf16[2,1024,256]{2,1,0:T(8,128)(2,1)S(1)}, bf16[2,1024,256]{2,1,0:T(8,128)(2,1)}, u32[]{:S(2)}) copy-start(bf16[2,1024,256]{2,1,0:T(8,128)(2,1)} %keys_ref.1) | copy-start | bytes 3145732
  93.5 34.4 %copy-start.2 = (bf16[2,1024,256]{2,1,0:T(8,128)(2,1)S(1)}, bf16[2,1024,256]{2,1,0:T(8,128)(2,1)}, u32[]{:S(2)}) copy-start(bf16[2,1024,256]{2,1,0:T(8,128)(2,1)} %values_ref.1) | copy-start | bytes 3145732
  93.5 34.4 %copy-start.4 = (s32[2]{0:T(128)S(1)}, s32[2]{0:T(128)}, u32[]{:S(2)}) copy-start(s32[2]{0:T(128)} %lengths_ref.1) | copy-start | bytes 28
  93.5 32.8 %all-to-all-start.2 = ((f32[64,16,128]{2,1,0:T(8,128)}), f32[64,16,128]{2,1,0:T(8,128)}, u32[]{:S(2)}, u32[]{:S(2)}) async-start(f32[64,16,128]{2,1,0:T(8,128)} %bitcast.36), calls=%async_computation.2 | async-start | bytes 1048576 | tf_op jit(solution)/shard_map/all_to_all | solution.py:199

commit v5 on v4

--- a/solution.py
+++ b/solution.py
@@ -9,9 +9,9 @@
 from jax.sharding import PartitionSpec as P
 
 SIDE = 8
+
+
 LANES = 128
-NEAR = 3
-FAR = SIDE - NEAR
 
 
 def times(rows, weights):
@@ -20,14 +20,15 @@
     )
 
 
-def near_body(
-    planes, own_rows, core_ref, gathered_ref, below_ref, own_ref, above_ref, pair_ref,
-    rows_ref, other_ref, same_ref, held,
+def strip_body(
+    planes, own_rows, core_ref, gathered_ref, *refs,
 ):
+    *pieces, other_ref, same_ref, held = refs
     at = 0
-    for piece in (below_ref, own_ref, above_ref, pair_ref):
+    for piece in pieces:
         held[at : at + piece.shape[0], :] = piece[...]
         at += piece.shape[0]
+    held[at:, :] = jnp.zeros((held.shape[0] - at, held.shape[1]), held.dtype)
     count = gathered_ref.shape[0]
     half = count // 2
     row_bits, x_bits = own_rows.bit_length() - 1, SIDE.bit_length() - 1
@@ -43,68 +44,30 @@
     pick = jnp.where(pick, 1.0, 0.0).astype(jnp.bfloat16)
     rows = jnp.dot(pick, gathered_ref[...], preferred_element_type=jnp.float32)
     rows = rows.astype(jnp.bfloat16)
-    rows_ref[...] = rows
     sums = times(rows, held[...])
     other_ref[...] = sums[:half]
     same_ref[...] = sums[half:]
 
 
-def near_sums(planes, own_rows, core, gathered, *pieces):
+def strip_sums(planes, own_rows, core, gathered, *pieces):
     count, width = gathered.shape
-    columns = sum(piece.shape[0] for piece in pieces)
+    columns = -(-sum(piece.shape[0] for piece in pieces) // LANES) * LANES
     product = jax.ShapeDtypeStruct((count // 2, columns), jnp.float32)
     in_vmem = pl.BlockSpec(memory_space=pltpu.VMEM)
     return pl.pallas_call(
-        functools.partial(near_body, planes, own_rows),
+        functools.partial(strip_body, planes, own_rows),
         in_specs=[pl.BlockSpec(memory_space=pltpu.SMEM)] + [in_vmem] * (1 + len(pieces)),
-        out_specs=[in_vmem] * 3,
-        out_shape=[jax.ShapeDtypeStruct(gathered.shape, gathered.dtype), product, product],
+        out_specs=[in_vmem] * 2,
+        out_shape=[product, product],
         scratch_shapes=[pltpu.VMEM((columns, width), jnp.bfloat16)],
-        compiler_params=pltpu.CompilerParams(vmem_limit_bytes=16 * 2**20),
+        compiler_params=pltpu.CompilerParams(vmem_limit_bytes=24 * 2**20),
         cost_estimate=pl.CostEstimate(
             flops=2 * count * width * (columns + count),
             bytes_accessed=2 * width * (2 * count + columns) + 4 * count * columns,
             transcendentals=0,
         ),
-        name="near_sums",
+        name="strip_sums",
     )(core.reshape(1), gathered, *pieces)
-
-
-def far_body(blocks, rows_ref, *refs):
-    *pieces, other_ref, same_ref, held = refs
-    half = rows_ref.shape[0] // 2
-    at = 0
-    for piece in pieces:
-        held[at : at + piece.shape[0], :] = piece[...]
-        at += piece.shape[0]
-    held[at:, :] = jnp.zeros((held.shape[0] - at, held.shape[1]), held.dtype)
-    sums = times(rows_ref[...], held[...])
-    for block in range(blocks):
-        lanes = slice(block * LANES, (block + 1) * LANES)
-        place = pl.ds(block, half, stride=blocks)
-        other_ref[place, :] = sums[:half, lanes]
-        same_ref[place, :] = sums[half:, lanes]
-
-
-def far_sums(rows, *pieces):
-    half, width = rows.shape[0] // 2, rows.shape[1]
-    blocks = -(-sum(piece.shape[0] for piece in pieces) // LANES)
-    product = jax.ShapeDtypeStruct((half * blocks, LANES), jnp.float32)
-    in_vmem = pl.BlockSpec(memory_space=pltpu.VMEM)
-    return pl.pallas_call(
-        functools.partial(far_body, blocks),
-        in_specs=[in_vmem] * (1 + len(pieces)),
-        out_specs=[in_vmem, in_vmem],
-        out_shape=[product, product],
-        scratch_shapes=[pltpu.VMEM((blocks * LANES, width), jnp.bfloat16)],
-        compiler_params=pltpu.CompilerParams(vmem_limit_bytes=20 * 2**20),
-        cost_estimate=pl.CostEstimate(
-            flops=4 * half * width * blocks * LANES,
-            bytes_accessed=2 * width * (2 * half + blocks * LANES) + 8 * half * blocks * LANES,
-            transcendentals=0,
-        ),
-        name="far_sums",
-    )(rows, *pieces)
 
 
 def attend_body(lengths_ref, queries_ref, pairs_ref, keys_ref, values_ref, out_ref):
@@ -176,6 +139,7 @@
 
     below = [lax.ppermute(q_weight, "mx", shift_y(1))]
     above = [lax.ppermute(q_weight, "mx", shift_y(-1))]
+    tokens, below[0], above[0] = lax.optimization_barrier((tokens, below[0], above[0]))
     copies = jnp.broadcast_to(tokens, (SIDE, *tokens.shape))
     gathered = lax.all_to_all(
         copies, "mx", split_axis=0, concat_axis=0, axis_index_groups=x_rings
@@ -202,18 +166,14 @@
         sums = jnp.sum(parts.reshape(planes, SIDE, *parts.shape[1:]), axis=0)
         return sums.astype(jnp.bfloat16).reshape(SIDE, own_rows, -1)
 
-    rows, *near = near_sums(
-        planes, own_rows, core, gathered, below[0].T, q_weight.T, above[0].T, pair_weight.T
+    pieces = (
+        below[0], q_weight, above[0], above[1], above[2], *opposite, below[2], below[1], pair_weight
     )
-    near = exchange(chip_sums(*near))
-    new_pairs = near[:, :, NEAR * columns :].transpose(1, 0, 2).reshape(own_rows, -1)
-    near = near[:, :, : NEAR * columns].transpose(1, 0, 2)
-    pieces = above[1], above[2], *opposite, below[2], below[1]
-    far = chip_sums(*far_sums(rows, *(piece.T for piece in pieces)))
-    far, near, new_pairs = lax.optimization_barrier((far, near, new_pairs))
-    far = exchange(far)
-    far = far[:, :, : FAR * columns].transpose(1, 0, 2)
-    query_rows = jnp.concatenate([near, far], axis=2).reshape(own_rows, SIDE, SIDE, columns)
+    sums = strip_sums(planes, own_rows, core, gathered, *(piece.T for piece in pieces))
+    strip = exchange(chip_sums(*sums))
+    new_pairs = strip[:, :, SIDE * columns : SIDE * columns + pair_columns].transpose(1, 0, 2).reshape(own_rows, -1)
+    query_rows = strip[:, :, : SIDE * columns].transpose(1, 0, 2)
+    query_rows = query_rows.reshape(own_rows, SIDE, SIDE, columns)
     query_rows = jnp.concatenate([query_rows, query_rows], axis=2)
     query_rows = lax.dynamic_slice_in_dim(query_rows, (SIDE + 1 - y_index) % SIDE, SIDE, 2)
     queries = query_rows.reshape(own_rows, -1, head_size)

time: 131 us -> 126 us (0.962)
  starting transfers between devices: 73.4 us -> 55.1 us
  waiting for transfers between devices: 43.5 us -> 54.2 us
  local copies, waits for them, and re-layouts: 4.31 us -> 9.72 us
  Pallas kernels: 6.14 us -> 4.23 us
    all_to_all x2 -> x1, starting transfers between devices: 35.4 us -> 17.8 us  [exchange(): lax.all_to_all(sums, ('mx', 'my'), split_axis=0, concat_axis=0, axis_inde...]
    ppermute x1, waiting for transfers between devices: 0.01 us -> 7.83 us  [local(): below = [lax.ppermute(q_weight, 'mx', shift_y(1))]]
    all_to_all x2 -> x1, waiting for transfers between devices: 19.7 us -> 25.5 us  [exchange(): lax.all_to_all(sums, ('mx', 'my'), split_axis=0, concat_axis=0, axis_inde...]
    ppermute x1, starting transfers between devices: 1.92 us -> 5.34 us  [local(): lax.ppermute(above[2][:, half:], 'mx', shift_y(-1))]
    unnamed x13 -> x21, local copies, waits for them, and re-layouts: 0.85 us -> 3.85 us
    ppermute x1, waiting for transfers between devices: 7.64 us -> 5.18 us  [local(): above = [lax.ppermute(q_weight, 'mx', shift_y(-1))]]
    ppermute x2, starting transfers between devices: 7.52 us -> 5.17 us  [local(): below.append(lax.ppermute(below[-1], 'mx', shift_y(1)))]
    pallas_call x2 -> x1, Pallas kernels: 4.75 us -> 2.84 us  [strip_sums(): pl.pallas_call(functools.partial(strip_body, planes, own_rows), in_specs=...]
  transfers between devices with their start and end apart: 13 -> 11, of which waited for: 6 -> 6; matrix products, arithmetic and copies ran while one was open for 1% -> 4% of each run, Pallas kernels for 4% -> 0%
where the time goes in v5:
time: 126 us; the launch traced here: 125 us
  starting transfers between devices  55.1 us (44%)
  waiting for transfers between devices  54.2 us (43%)
  local copies, waits for them, and re-layouts  9.72 us (8%)
  Pallas kernels  4.23 us (3%)
  other arithmetic  1.62 us (1%)
    all_to_all x1, waiting for transfers between devices, exchange(): lax.all_to_all(sums, ('mx', 'my'), split_axis=0, concat_axis=0, axis_inde...  25.5 us
    all_to_all x1, starting transfers between devices, exchange(): lax.all_to_all(sums, ('mx', 'my'), split_axis=0, concat_axis=0, axis_inde...  17.8 us
    ppermute x1, waiting for transfers between devices, local(): below = [lax.ppermute(q_weight, 'mx', shift_y(1))]  7.83 us
    ppermute x1, waiting for transfers between devices, local(): lax.ppermute(above[2][:, half:], 'mx', shift_y(-1))  7.26 us
    all_to_all x1, starting transfers between devices, local(): lax.all_to_all(copies, 'mx', split_axis=0, concat_axis=0, axis_index_grou...  6.76 us
    ppermute x2, starting transfers between devices, local(): above.append(lax.ppermute(above[-1], 'mx', shift_y(-1)))  6.63 us
    ppermute x2, waiting for transfers between devices, local(): below.append(lax.ppermute(below[-1], 'mx', shift_y(1)))  6.08 us
    ppermute x1, starting transfers between devices, local(): lax.ppermute(above[2][:, half:], 'mx', shift_y(-1))  5.34 us
  transfers between devices with their start and end apart: 11, of which 6 were waited for; matrix products, arithmetic and copies ran while one was open for 4% of the time, Pallas kernels for 0%

profile of v5, /device:TPU:48, one launch (start us, length us, event | category | flops | bytes accessed | tf_op | source)
XLA Modules:
  0.0 125.2 jit_solution(14819295155634973611)
XLA Ops:
  0.0 0.0 copy-start
  0.0 4.9 %collective-permute-start = (bf16[1152,192]{0,1:T(8,128)(2,1)}, bf16[1152,192]{0,1:T(8,128)(2,1)S(1)}, u32[]{:S(2)}, u32[]{:S(2)}) collective-permute-start(bf16[1152,192]{0,1:T(8,128)(2,1)} %param.7), channel_id=1, source_target_pairs={{0,16},{16,32},{32,48},{48,64},{64,80},{80,96},{96,112},{112,0},{1... | collective-permute-start | bytes 1327112 | tf_op jit(solution)/shard_map/ppermute | solution.py:140
  4.9 1.9 %collective-permute-start.1 = (bf16[1152,192]{0,1:T(8,128)(2,1)}, bf16[1152,192]{0,1:T(8,128)(2,1)S(1)}, u32[]{:S(2)}, u32[]{:S(2)}) collective-permute-start(bf16[1152,192]{0,1:T(8,128)(2,1)} %param.7), channel_id=1, source_target_pairs={{0,112},{16,0},{32,16},{48,32},{64,48},{80,64},{96,80},{112,96},{1... | collective-permute-start | bytes 1327112 | tf_op jit(solution)/shard_map/ppermute | solution.py:141
  6.9 7.8 %collective-permute-done = bf16[1152,192]{0,1:T(8,128)(2,1)S(1)} collective-permute-done((bf16[1152,192]{0,1:T(8,128)(2,1)}, bf16[1152,192]{0,1:T(8,128)(2,1)S(1)}, u32[]{:S(2)}, u32[]{:S(2)}) %collective-permute-start) | collective-permute-done | bytes 442400 | tf_op jit(solution)/shard_map/ppermute | solution.py:140
  14.7 5.2 %collective-permute-done.1 = bf16[1152,192]{0,1:T(8,128)(2,1)S(1)} collective-permute-done((bf16[1152,192]{0,1:T(8,128)(2,1)}, bf16[1152,192]{0,1:T(8,128)(2,1)S(1)}, u32[]{:S(2)}, u32[]{:S(2)}) %collective-permute-start.1) | collective-permute-done | bytes 442400 | tf_op jit(solution)/shard_map/ppermute | solution.py:141
  19.9 1.9 %collective-permute-start.4 = (bf16[1152,192]{0,1:T(8,128)(2,1)S(1)}, bf16[1152,192]{0,1:T(8,128)(2,1)}, u32[]{:S(2)}, u32[]{:S(2)}) collective-permute-start(bf16[1152,192]{0,1:T(8,128)(2,1)S(1)} %collective-permute-done), channel_id=1, source_target_pairs={{0,16},{16,32},{32,48},{48,64},{64,80},{80,96},{96,112},{112,0},{1... | collective-permute-start | bytes 1327112 | tf_op jit(solution)/shard_map/ppermute | solution.py:148
  21.8 3.9 %collective-permute-start.2 = (bf16[1152,192]{0,1:T(8,128)(2,1)S(1)}, bf16[1152,192]{0,1:T(8,128)(2,1)}, u32[]{:S(2)}, u32[]{:S(2)}) collective-permute-start(bf16[1152,192]{0,1:T(8,128)(2,1)S(1)} %collective-permute-done.1), channel_id=1, source_target_pairs={{0,112},{16,0},{32,16},{48,32},{64,48},{80,64},{96,80},{112,96},{1... | collective-permute-start | bytes 1327112 | tf_op jit(solution)/shard_map/ppermute | solution.py:149
  25.7 1.8 %broadcast_in_dim.3 = bf16[8,32,1152]{2,1,0:T(8,128)(2,1)} broadcast(bf16[32,1152]{1,0:T(8,128)(2,1)} %param.6), dimensions={1,2} | broadcast | bytes 663552 | tf_op jit(solution)/shard_map/broadcast_in_dim | solution.py:143
  27.5 6.8 %all-to-all-start = ((bf16[8,32,1152]{2,1,0:T(8,128)(2,1)}), bf16[8,32,1152]{2,1,0:T(8,128)(2,1)S(1)}, u32[]{:S(2)}, u32[]{:S(2)}) async-start(bf16[8,32,1152]{2,1,0:T(8,128)(2,1)} %broadcast_in_dim.3), calls=%async_computation | async-start | bytes 1179648 | tf_op jit(solution)/shard_map/all_to_all | solution.py:144
  34.3 0.0 copy-done.4
  34.3 0.0 copy-start.3
  34.3 0.0 collective-permute-done.4
  34.3 3.3 %collective-permute-start.5 = (bf16[1152,192]{0,1:T(8,128)(2,1)}, bf16[1152,192]{0,1:T(8,128)(2,1)S(1)}, u32[]{:S(2)}, u32[]{:S(2)}) collective-permute-start(bf16[1152,192]{0,1:T(8,128)(2,1)} %collective-permute-done.4), channel_id=1, source_target_pairs={{0,16},{16,32},{32,48},{48,64},{64,80},{80,96},{96,112},{112,0},{1... | collective-permute-start | bytes 1327112 | tf_op jit(solution)/shard_map/ppermute | solution.py:148
  37.6 0.0 copy-done.6
  37.6 0.0 collective-permute-done.2
  37.6 2.7 %collective-permute-start.3 = (bf16[1152,192]{0,1:T(8,128)(2,1)}, bf16[1152,192]{0,1:T(8,128)(2,1)S(1)}, u32[]{:S(2)}, u32[]{:S(2)}) collective-permute-start(bf16[1152,192]{0,1:T(8,128)(2,1)} %collective-permute-done.2), channel_id=1, source_target_pairs={{0,112},{16,0},{32,16},{48,32},{64,48},{80,64},{96,80},{112,96},{1... | collective-permute-start | bytes 1327112 | tf_op jit(solution)/shard_map/ppermute | solution.py:149
  40.3 6.1 %collective-permute-done.5 = bf16[1152,192]{0,1:T(8,128)(2,1)S(1)} collective-permute-done((bf16[1152,192]{0,1:T(8,128)(2,1)}, bf16[1152,192]{0,1:T(8,128)(2,1)S(1)}, u32[]{:S(2)}, u32[]{:S(2)}) %collective-permute-start.5) | collective-permute-done | bytes 442400 | tf_op jit(solution)/shard_map/ppermute | solution.py:148
  46.4 0.7 slice.16
  47.1 4.6 %collective-permute-start.6 = (bf16[1152,96]{0,1:T(8,128)(2,1)}, bf16[1152,96]{0,1:T(8,128)(2,1)S(1)}, u32[]{:S(2)}, u32[]{:S(2)}) collective-permute-start(bf16[1152,96]{0,1:T(8,128)(2,1)} %slice.16), channel_id=1, source_target_pairs={{0,16},{16,32},{32,48},{48,64},{64,80},{80,96},{96,112},{112,0},{1... | collective-permute-start | bytes 663560 | tf_op jit(solution)/shard_map/ppermute | solution.py:152
  51.7 0.0 collective-permute-done.3
  51.7 0.7 slice.17
  52.4 5.3 %collective-permute-start.7 = (bf16[1152,96]{0,1:T(8,128)(2,1)}, bf16[1152,96]{0,1:T(8,128)(2,1)}, u32[]{:S(2)}, u32[]{:S(2)}) collective-permute-start(bf16[1152,96]{0,1:T(8,128)(2,1)} %slice.17), channel_id=1, source_target_pairs={{0,112},{16,0},{32,16},{48,32},{64,48},{80,64},{96,80},{112,96},{1... | collective-permute-start | bytes 663560 | tf_op jit(solution)/shard_map/ppermute | solution.py:153
  57.8 0.0 copy-done
  57.8 0.9 constant_dynamic-slice_fusion
  58.7 1.1 copy.13
  59.8 0.0 all-to-all-done
  59.8 0.0 collective-permute-done.6
  59.8 7.3 %collective-permute-done.7 = bf16[1152,96]{0,1:T(8,128)(2,1)} collective-permute-done((bf16[1152,96]{0,1:T(8,128)(2,1)}, bf16[1152,96]{0,1:T(8,128)(2,1)}, u32[]{:S(2)}, u32[]{:S(2)}) %collective-permute-start.7) | collective-permute-done | bytes 221216 | tf_op jit(solution)/shard_map/ppermute | solution.py:153
  67.1 0.0 copy-done.3
  67.1 1.0 copy-done.5
  68.1 1.0 copy-done.7
  69.1 2.8 %strip_sums.1 = (f32[128,1664]{1,0:T(8,128)S(1)}, f32[128,1664]{1,0:T(8,128)S(1)}) custom-call(s32[1]{0:T(128)} %bitcast.core_ref, bf16[256,1152]{1,0:T(8,128)(2,1)S(1)} %bitcast.23, bf16[192,1152]{1,0:T(8,128)(2,1)S(1)} %bitcast.28, bf16[192,1152]{1,0:T(8,128)(2,1)S(1)} %bitcast.27, bf16[192,1152]{1,0:T(8,128)(2,1)S(1)} %bitcast.29, ...), custom_call_target="tpu_custom_call" | custom-call | flops 1132462080 | bytes 6717440 | tf_op jit(solution)/shard_map/strip_sums/pallas_call | solution.py:57
  72.0 1.9 %collective-permute-start.8 = (f32[128,1664]{1,0:T(8,128)S(1)}, f32[128,1664]{1,0:T(8,128)S(1)}, u32[]{:S(2)}, u32[]{:S(2)}) collective-permute-start(f32[128,1664]{1,0:T(8,128)S(1)} %get-tuple-element.14), channel_id=1, source_target_pairs={{0,1},{1,0},{2,3},{3,2},{4,5},{5,4},{6,7},{7,6},{8,9},{9,8},{10,11... | collective-permute-start | bytes 2555912 | tf_op jit(solution)/shard_map/ppermute | solution.py:159
  73.9 2.3 %collective-permute-done.8 = f32[128,1664]{1,0:T(8,128)S(1)} collective-permute-done((f32[128,1664]{1,0:T(8,128)S(1)}, f32[128,1664]{1,0:T(8,128)S(1)}, u32[]{:S(2)}, u32[]{:S(2)}) %collective-permute-start.8) | collective-permute-done | bytes 852000 | tf_op jit(solution)/shard_map/ppermute | solution.py:159
  76.2 0.1 add.22
  76.3 1.5 %reshape.26 = f32[64,2,1664]{2,1,0:T(2,128)} reshape(f32[128,1664]{1,0:T(8,128)S(1)} %add.22) | data formatting | bytes 1703936 | tf_op jit(solution)/shard_map/reshape | solution.py:160
  77.8 17.8 %all-to-all-start.1 = ((f32[64,2,1664]{2,1,0:T(2,128)}), f32[64,2,1664]{2,1,0:T(2,128)}, u32[]{:S(2)}, u32[]{:S(2)}) async-start(f32[64,2,1664]{2,1,0:T(2,128)} %reshape.26), calls=%async_computation.1 | async-start | bytes 1703936 | tf_op jit(solution)/shard_map/all_to_all | solution.py:163
  95.6 0.0 copy-start.1
  95.6 0.0 copy-start.8
  95.7 25.5 %all-to-all-done.1 = f32[64,2,1664]{2,1,0:T(2,128)} async-done(((f32[64,2,1664]{2,1,0:T(2,128)}), f32[64,2,1664]{2,1,0:T(2,128)}, u32[]{:S(2)}, u32[]{:S(2)}) %all-to-all-start.1) | async-done | bytes 852000 | tf_op jit(solution)/shard_map/all_to_all | solution.py:163
  121.2 1.5 %reduce_sum.9 = bf16[8,2,1664]{2,1,0:T(2,128)(2,1)S(1)} reduce(f32[8,8,2,1664]{3,2,1,0:T(2,128)} %bitcast.12, f32[]{:T(128)} %constant.55.clone.1), dimensions={0}, to_apply=%region_0.1 | reduce | flops 186368 | bytes 905220 | tf_op jit(solution)/shard_map/reduce_sum | solution.py:166
  122.7 0.1 reshape.30.pairs_ref
  122.8 0.1 reshape.28
  122.9 0.1 fusion
  123.0 0.1 reshape.29.queries_ref
  123.2 0.0 copy-done.2
  123.2 1.4 %attend.1 = bf16[2,48,256]{2,1,0:T(8,128)(2,1)S(1)} custom-call(s32[2]{0:T(128)S(1)} %copy-done.8, bf16[2,48,256]{2,1,0:T(8,128)(2,1)S(1)} %reshape.29.queries_ref, bf16[2,512]{1,0:T(2,128)(2,1)S(1)} %reshape.30.pairs_ref, bf16[2,1024,256]{2,1,0:T(8,128)(2,1)S(1)} %copy-done.1, bf16[2,1024,256]{2,1,0:T(8,128)(2,1)S(1)} %copy-done.2), custom_call_target="tpu_custom_call" | custom-call | flops 100663296 | bytes 2097152 | tf_op jit(solution)/shard_map/attend/pallas_call | solution.py:100
  124.6 0.7 copy.15
  (11 shorter events, 0.1 us)
Async XLA Ops:
  0.0 57.8 %copy-start = (bf16[1152,512]{1,0:T(8,128)(2,1)S(1)}, bf16[1152,512]{1,0:T(8,128)(2,1)}, u32[]{:S(2)}) copy-start(bf16[1152,512]{1,0:T(8,128)(2,1)} %param.8) | copy-start | bytes 3538948
  0.0 14.7 %collective-permute-start = (bf16[1152,192]{0,1:T(8,128)(2,1)}, bf16[1152,192]{0,1:T(8,128)(2,1)S(1)}, u32[]{:S(2)}, u32[]{:S(2)}) collective-permute-start(bf16[1152,192]{0,1:T(8,128)(2,1)} %param.7), channel_id=1, source_target_pairs={{0,16},{16,32},{32,48},{48,64},{64,80},{80,96},{96,112},{112,0},{1... | collective-permute-start | bytes 1327112 | tf_op jit(solution)/shard_map/ppermute | solution.py:140
  4.9 14.9 %collective-permute-start.1 = (bf16[1152,192]{0,1:T(8,128)(2,1)}, bf16[1152,192]{0,1:T(8,128)(2,1)S(1)}, u32[]{:S(2)}, u32[]{:S(2)}) collective-permute-start(bf16[1152,192]{0,1:T(8,128)(2,1)} %param.7), channel_id=1, source_target_pairs={{0,112},{16,0},{32,16},{48,32},{64,48},{80,64},{96,80},{112,96},{1... | collective-permute-start | bytes 1327112 | tf_op jit(solution)/shard_map/ppermute | solution.py:141
  14.7 19.5 %copy-start.4 = (bf16[1152,192]{0,1:T(8,128)(2,1)}, bf16[1152,192]{0,1:T(8,128)(2,1)S(1)}, u32[]{:S(2)}) copy-start(bf16[1152,192]{0,1:T(8,128)(2,1)S(1)} %collective-permute-done) | copy-start | bytes 1327108
  19.9 17.7 %copy-start.6 = (bf16[1152,192]{0,1:T(8,128)(2,1)}, bf16[1152,192]{0,1:T(8,128)(2,1)S(1)}, u32[]{:S(2)}) copy-start(bf16[1152,192]{0,1:T(8,128)(2,1)S(1)} %collective-permute-done.1) | copy-start | bytes 1327108
  19.9 14.4 %collective-permute-start.4 = (bf16[1152,192]{0,1:T(8,128)(2,1)S(1)}, bf16[1152,192]{0,1:T(8,128)(2,1)}, u32[]{:S(2)}, u32[]{:S(2)}) collective-permute-start(bf16[1152,192]{0,1:T(8,128)(2,1)S(1)} %collective-permute-done), channel_id=1, source_target_pairs={{0,16},{16,32},{32,48},{48,64},{64,80},{80,96},{96,112},{112,0},{1... | collective-permute-start | bytes 1327112 | tf_op jit(solution)/shard_map/ppermute | solution.py:148
  21.8 15.8 %collective-permute-start.2 = (bf16[1152,192]{0,1:T(8,128)(2,1)S(1)}, bf16[1152,192]{0,1:T(8,128)(2,1)}, u32[]{:S(2)}, u32[]{:S(2)}) collective-permute-start(bf16[1152,192]{0,1:T(8,128)(2,1)S(1)} %collective-permute-done.1), channel_id=1, source_target_pairs={{0,112},{16,0},{32,16},{48,32},{64,48},{80,64},{96,80},{112,96},{1... | collective-permute-start | bytes 1327112 | tf_op jit(solution)/shard_map/ppermute | solution.py:149
  27.5 32.3 %all-to-all-start = ((bf16[8,32,1152]{2,1,0:T(8,128)(2,1)}), bf16[8,32,1152]{2,1,0:T(8,128)(2,1)S(1)}, u32[]{:S(2)}, u32[]{:S(2)}) async-start(bf16[8,32,1152]{2,1,0:T(8,128)(2,1)} %broadcast_in_dim.3), calls=%async_computation | async-start | bytes 1179648 | tf_op jit(solution)/shard_map/all_to_all | solution.py:144
  34.3 32.8 %copy-start.3 = (bf16[1152,192]{0,1:T(8,128)(2,1)S(1)}, bf16[1152,192]{0,1:T(8,128)(2,1)}, u32[]{:S(2)}) copy-start(bf16[1152,192]{0,1:T(8,128)(2,1)} %param.7) | copy-start | bytes 1327108
  34.3 12.1 %collective-permute-start.5 = (bf16[1152,192]{0,1:T(8,128)(2,1)}, bf16[1152,192]{0,1:T(8,128)(2,1)S(1)}, u32[]{:S(2)}, u32[]{:S(2)}) collective-permute-start(bf16[1152,192]{0,1:T(8,128)(2,1)} %collective-permute-done.4), channel_id=1, source_target_pairs={{0,16},{16,32},{32,48},{48,64},{64,80},{80,96},{96,112},{112,0},{1... | collective-permute-start | bytes 1327112 | tf_op jit(solution)/shard_map/ppermute | solution.py:148
  37.6 14.1 %collective-permute-start.3 = (bf16[1152,192]{0,1:T(8,128)(2,1)}, bf16[1152,192]{0,1:T(8,128)(2,1)S(1)}, u32[]{:S(2)}, u32[]{:S(2)}) collective-permute-start(bf16[1152,192]{0,1:T(8,128)(2,1)} %collective-permute-done.2), channel_id=1, source_target_pairs={{0,112},{16,0},{32,16},{48,32},{64,48},{80,64},{96,80},{112,96},{1... | collective-permute-start | bytes 1327112 | tf_op jit(solution)/shard_map/ppermute | solution.py:149
  47.1 12.7 %collective-permute-start.6 = (bf16[1152,96]{0,1:T(8,128)(2,1)}, bf16[1152,96]{0,1:T(8,128)(2,1)S(1)}, u32[]{:S(2)}, u32[]{:S(2)}) collective-permute-start(bf16[1152,96]{0,1:T(8,128)(2,1)} %slice.16), channel_id=1, source_target_pairs={{0,16},{16,32},{32,48},{48,64},{64,80},{80,96},{96,112},{112,0},{1... | collective-permute-start | bytes 663560 | tf_op jit(solution)/shard_map/ppermute | solution.py:152
  52.4 14.6 %collective-permute-start.7 = (bf16[1152,96]{0,1:T(8,128)(2,1)}, bf16[1152,96]{0,1:T(8,128)(2,1)}, u32[]{:S(2)}, u32[]{:S(2)}) collective-permute-start(bf16[1152,96]{0,1:T(8,128)(2,1)} %slice.17), channel_id=1, source_target_pairs={{0,112},{16,0},{32,16},{48,32},{64,48},{80,64},{96,80},{112,96},{1... | collective-permute-start | bytes 663560 | tf_op jit(solution)/shard_map/ppermute | solution.py:153
  67.1 1.0 copy-start.5
  68.1 1.0 copy-start.7
  72.0 4.3 %collective-permute-start.8 = (f32[128,1664]{1,0:T(8,128)S(1)}, f32[128,1664]{1,0:T(8,128)S(1)}, u32[]{:S(2)}, u32[]{:S(2)}) collective-permute-start(f32[128,1664]{1,0:T(8,128)S(1)} %get-tuple-element.14), channel_id=1, source_target_pairs={{0,1},{1,0},{2,3},{3,2},{4,5},{5,4},{6,7},{7,6},{8,9},{9,8},{10,11... | collective-permute-start | bytes 2555912 | tf_op jit(solution)/shard_map/ppermute | solution.py:159
  77.8 45.4 %copy-start.2 = (bf16[2,1024,256]{2,1,0:T(8,128)(2,1)S(1)}, bf16[2,1024,256]{2,1,0:T(8,128)(2,1)}, u32[]{:S(2)}) copy-start(bf16[2,1024,256]{2,1,0:T(8,128)(2,1)} %values_ref.1) | copy-start | bytes 3145732
  77.8 43.4 %all-to-all-start.1 = ((f32[64,2,1664]{2,1,0:T(2,128)}), f32[64,2,1664]{2,1,0:T(2,128)}, u32[]{:S(2)}, u32[]{:S(2)}) async-start(f32[64,2,1664]{2,1,0:T(2,128)} %reshape.26), calls=%async_computation.1 | async-start | bytes 1703936 | tf_op jit(solution)/shard_map/all_to_all | solution.py:163
  95.6 27.5 %copy-start.1 = (bf16[2,1024,256]{2,1,0:T(8,128)(2,1)S(1)}, bf16[2,1024,256]{2,1,0:T(8,128)(2,1)}, u32[]{:S(2)}) copy-start(bf16[2,1024,256]{2,1,0:T(8,128)(2,1)} %keys_ref.1) | copy-start | bytes 3145732
  95.6 27.5 %copy-start.8 = (s32[2]{0:T(128)S(1)}, s32[2]{0:T(128)}, u32[]{:S(2)}) copy-start(s32[2]{0:T(128)} %lengths_ref.1) | copy-start | bytes 28

commit v6 on v5

--- a/solution.py
+++ b/solution.py
@@ -28,7 +28,8 @@
     for piece in pieces:
         held[at : at + piece.shape[0], :] = piece[...]
         at += piece.shape[0]
-    held[at:, :] = jnp.zeros((held.shape[0] - at, held.shape[1]), held.dtype)
+    if at < held.shape[0]:
+        held[at:, :] = jnp.zeros((held.shape[0] - at, held.shape[1]), held.dtype)
     count = gathered_ref.shape[0]
     half = count // 2
     row_bits, x_bits = own_rows.bit_length() - 1, SIDE.bit_length() - 1
@@ -166,13 +167,23 @@
         sums = jnp.sum(parts.reshape(planes, SIDE, *parts.shape[1:]), axis=0)
         return sums.astype(jnp.bfloat16).reshape(SIDE, own_rows, -1)
 
-    pieces = (
-        below[0], q_weight, above[0], above[1], above[2], *opposite, below[2], below[1], pair_weight
-    )
-    sums = strip_sums(planes, own_rows, core, gathered, *(piece.T for piece in pieces))
-    strip = exchange(chip_sums(*sums))
-    new_pairs = strip[:, :, SIDE * columns : SIDE * columns + pair_columns].transpose(1, 0, 2).reshape(own_rows, -1)
-    query_rows = strip[:, :, : SIDE * columns].transpose(1, 0, 2)
+    near = below[0], q_weight, above[0], above[1], below[1], pair_weight
+    far = above[2], *opposite, below[2]
+    near, far = (
+        chip_sums(*strip_sums(planes, own_rows, core, gathered, *(piece.T for piece in pieces)))
+        for pieces in (near, far)
+    )
+    far_at = near.shape[2]
+    strip = exchange(jnp.concatenate([near, far], axis=2)).transpose(1, 0, 2)
+    new_pairs = strip[:, :, 5 * columns : 5 * columns + pair_columns].reshape(own_rows, -1)
+    query_rows = jnp.concatenate(
+        [
+            strip[:, :, : 4 * columns],
+            strip[:, :, far_at : far_at + 3 * columns],
+            strip[:, :, 4 * columns : 5 * columns],
+        ],
+        axis=2,
+    )
     query_rows = query_rows.reshape(own_rows, SIDE, SIDE, columns)
     query_rows = jnp.concatenate([query_rows, query_rows], axis=2)
     query_rows = lax.dynamic_slice_in_dim(query_rows, (SIDE + 1 - y_index) % SIDE, SIDE, 2)

time: 126 us -> 127 us (level)
  waiting for transfers between devices: 54.2 us -> 46.2 us
  starting transfers between devices: 55.1 us -> 62.3 us
  Pallas kernels: 4.23 us -> 6.5 us
  local copies, waits for them, and re-layouts: 9.72 us -> 8.13 us
  other arithmetic: 1.62 us -> 2.95 us
    ppermute x1, waiting for transfers between devices: 7.26 us -> 0.01 us  [local(): lax.ppermute(above[2][:, half:], 'mx', shift_y(-1))]
    ppermute x2, waiting for transfers between devices: 0.01 us -> 6.2 us  [local(): above.append(lax.ppermute(above[-1], 'mx', shift_y(-1)))]
    ppermute x2, waiting for transfers between devices: 6.08 us -> 0.01 us  [local(): below.append(lax.ppermute(below[-1], 'mx', shift_y(1)))]
    all_to_all x1, starting transfers between devices: 17.8 us -> 23.2 us  [exchange(): lax.all_to_all(sums, ('mx', 'my'), split_axis=0, concat_axis=0, axis_inde...]
    ppermute x2, starting transfers between devices: 5.17 us -> 8.29 us  [local(): below.append(lax.ppermute(below[-1], 'mx', shift_y(1)))]
    ppermute x1 -> x2, starting transfers between devices: 1.92 us -> 4.32 us  [chip_sums(): swapped = lax.ppermute(other_sums, 'my', core_pairs)]
    pallas_call x1 -> x2, Pallas kernels: 2.84 us -> 5.1 us  [strip_sums(): pl.pallas_call(functools.partial(strip_body, planes, own_rows), in_specs=...]
    unnamed x21 -> x17, local copies, waits for them, and re-layouts: 3.85 us -> 1.87 us
  transfers between devices with their start and end apart: 11 -> 12, of which waited for: 6 -> 5; matrix products, arithmetic and copies ran while one was open for 4% -> 4% of each run, Pallas kernels for 0% -> 4%
where the time goes in v6:
time: 127 us
  starting transfers between devices  62.3 us (49%)
  waiting for transfers between devices  46.2 us (36%)
  local copies, waits for them, and re-layouts  8.13 us (6%)
  Pallas kernels  6.5 us (5%)
  other arithmetic  2.95 us (2%)
    all_to_all x1, waiting for transfers between devices, exchange(): lax.all_to_all(sums, ('mx', 'my'), split_axis=0, concat_axis=0, axis_inde...  25.8 us
    all_to_all x1, starting transfers between devices, exchange(): lax.all_to_all(sums, ('mx', 'my'), split_axis=0, concat_axis=0, axis_inde...  23.2 us
    ppermute x2, starting transfers between devices, local(): below.append(lax.ppermute(below[-1], 'mx', shift_y(1)))  8.29 us
    ppermute x1, waiting for transfers between devices, local(): below = [lax.ppermute(q_weight, 'mx', shift_y(1))]  7.83 us
    all_to_all x1, starting transfers between devices, local(): lax.all_to_all(copies, 'mx', split_axis=0, concat_axis=0, axis_index_grou...  6.76 us
    ppermute x2, waiting for transfers between devices, local(): above.append(lax.ppermute(above[-1], 'mx', shift_y(-1)))  6.2 us
    ppermute x2, starting transfers between devices, local(): above.append(lax.ppermute(above[-1], 'mx', shift_y(-1)))  5.94 us
    ppermute x1, waiting for transfers between devices, local(): above = [lax.ppermute(q_weight, 'mx', shift_y(-1))]  5.18 us
  transfers between devices with their start and end apart: 12, of which 5 were waited for; matrix products, arithmetic and copies ran while one was open for 4% of the time, Pallas kernels for 4%

profile of v6, /device:TPU:48, one launch (start us, length us, event | category | flops | bytes accessed | tf_op | source)
XLA Modules:
  0.0 126.5 jit_solution(746670966584401279)
XLA Ops:
  0.0 4.9 %collective-permute-start = (bf16[1152,192]{0,1:T(8,128)(2,1)}, bf16[1152,192]{0,1:T(8,128)(2,1)S(1)}, u32[]{:S(2)}, u32[]{:S(2)}) collective-permute-start(bf16[1152,192]{0,1:T(8,128)(2,1)} %param.7), channel_id=1, source_target_pairs={{0,16},{16,32},{32,48},{48,64},{64,80},{80,96},{96,112},{112,0},{1... | collective-permute-start | bytes 1327112 | tf_op jit(solution)/shard_map/ppermute | solution.py:141
  4.9 1.9 %collective-permute-start.1 = (bf16[1152,192]{0,1:T(8,128)(2,1)}, bf16[1152,192]{0,1:T(8,128)(2,1)S(1)}, u32[]{:S(2)}, u32[]{:S(2)}) collective-permute-start(bf16[1152,192]{0,1:T(8,128)(2,1)} %param.7), channel_id=1, source_target_pairs={{0,112},{16,0},{32,16},{48,32},{64,48},{80,64},{96,80},{112,96},{1... | collective-permute-start | bytes 1327112 | tf_op jit(solution)/shard_map/ppermute | solution.py:142
  6.9 7.8 %collective-permute-done = bf16[1152,192]{0,1:T(8,128)(2,1)S(1)} collective-permute-done((bf16[1152,192]{0,1:T(8,128)(2,1)}, bf16[1152,192]{0,1:T(8,128)(2,1)S(1)}, u32[]{:S(2)}, u32[]{:S(2)}) %collective-permute-start) | collective-permute-done | bytes 442400 | tf_op jit(solution)/shard_map/ppermute | solution.py:141
  14.7 5.2 %collective-permute-done.1 = bf16[1152,192]{0,1:T(8,128)(2,1)S(1)} collective-permute-done((bf16[1152,192]{0,1:T(8,128)(2,1)}, bf16[1152,192]{0,1:T(8,128)(2,1)S(1)}, u32[]{:S(2)}, u32[]{:S(2)}) %collective-permute-start.1) | collective-permute-done | bytes 442400 | tf_op jit(solution)/shard_map/ppermute | solution.py:142
  19.9 1.9 %collective-permute-start.2 = (bf16[1152,192]{0,1:T(8,128)(2,1)S(1)}, bf16[1152,192]{0,1:T(8,128)(2,1)}, u32[]{:S(2)}, u32[]{:S(2)}) collective-permute-start(bf16[1152,192]{0,1:T(8,128)(2,1)S(1)} %collective-permute-done.1), channel_id=1, source_target_pairs={{0,112},{16,0},{32,16},{48,32},{64,48},{80,64},{96,80},{112,96},{1... | collective-permute-start | bytes 1327112 | tf_op jit(solution)/shard_map/ppermute | solution.py:150
  21.8 5.1 %collective-permute-start.3 = (bf16[1152,192]{0,1:T(8,128)(2,1)S(1)}, bf16[1152,192]{0,1:T(8,128)(2,1)}, u32[]{:S(2)}, u32[]{:S(2)}) collective-permute-start(bf16[1152,192]{0,1:T(8,128)(2,1)S(1)} %collective-permute-done), channel_id=1, source_target_pairs={{0,16},{16,32},{32,48},{48,64},{64,80},{80,96},{96,112},{112,0},{1... | collective-permute-start | bytes 1327112 | tf_op jit(solution)/shard_map/ppermute | solution.py:149
  26.9 1.8 %broadcast_in_dim.3 = bf16[8,32,1152]{2,1,0:T(8,128)(2,1)} broadcast(bf16[32,1152]{1,0:T(8,128)(2,1)} %param.6), dimensions={1,2} | broadcast | bytes 663552 | tf_op jit(solution)/shard_map/broadcast_in_dim | solution.py:144
  28.7 6.8 %all-to-all-start = ((bf16[8,32,1152]{2,1,0:T(8,128)(2,1)}), bf16[8,32,1152]{2,1,0:T(8,128)(2,1)S(1)}, u32[]{:S(2)}, u32[]{:S(2)}) async-start(bf16[8,32,1152]{2,1,0:T(8,128)(2,1)} %broadcast_in_dim.3), calls=%async_computation | async-start | bytes 1179648 | tf_op jit(solution)/shard_map/all_to_all | solution.py:145
  35.5 0.0 collective-permute-done.2
  35.5 4.0 %collective-permute-start.5 = (bf16[1152,192]{0,1:T(8,128)(2,1)}, bf16[1152,192]{0,1:T(8,128)(2,1)}, u32[]{:S(2)}, u32[]{:S(2)}) collective-permute-start(bf16[1152,192]{0,1:T(8,128)(2,1)} %collective-permute-done.2), channel_id=1, source_target_pairs={{0,112},{16,0},{32,16},{48,32},{64,48},{80,64},{96,80},{112,96},{1... | collective-permute-start | bytes 1327112 | tf_op jit(solution)/shard_map/ppermute | solution.py:150
  39.5 0.0 collective-permute-done.3
  39.5 3.2 %collective-permute-start.6 = (bf16[1152,192]{0,1:T(8,128)(2,1)}, bf16[1152,192]{0,1:T(8,128)(2,1)}, u32[]{:S(2)}, u32[]{:S(2)}) collective-permute-start(bf16[1152,192]{0,1:T(8,128)(2,1)} %collective-permute-done.3), channel_id=1, source_target_pairs={{0,16},{16,32},{32,48},{48,64},{64,80},{80,96},{96,112},{112,0},{1... | collective-permute-start | bytes 1327112 | tf_op jit(solution)/shard_map/ppermute | solution.py:149
  42.7 6.2 %collective-permute-done.5 = bf16[1152,192]{0,1:T(8,128)(2,1)} collective-permute-done((bf16[1152,192]{0,1:T(8,128)(2,1)}, bf16[1152,192]{0,1:T(8,128)(2,1)}, u32[]{:S(2)}, u32[]{:S(2)}) %collective-permute-start.5) | collective-permute-done | bytes 442400 | tf_op jit(solution)/shard_map/ppermute | solution.py:150
  48.9 1.6 %slice.25 = bf16[1152,96]{0,1:T(8,128)(2,1)} slice(bf16[1152,192]{0,1:T(8,128)(2,1)} %collective-permute-done.5), slice={[0:1152], [96:192]} | slice | bytes 442368 | tf_op jit(solution)/shard_map/slice | solution.py:154
  50.5 3.5 %collective-permute-start.8 = (bf16[1152,96]{0,1:T(8,128)(2,1)}, bf16[1152,96]{0,1:T(8,128)(2,1)S(1)}, u32[]{:S(2)}, u32[]{:S(2)}) collective-permute-start(bf16[1152,96]{0,1:T(8,128)(2,1)} %slice.25), channel_id=1, source_target_pairs={{0,112},{16,0},{32,16},{48,32},{64,48},{80,64},{96,80},{112,96},{1... | collective-permute-start | bytes 663560 | tf_op jit(solution)/shard_map/ppermute | solution.py:154
  54.0 0.0 collective-permute-done.6
  54.0 1.6 %slice.24 = bf16[1152,96]{0,1:T(8,128)(2,1)} slice(bf16[1152,192]{0,1:T(8,128)(2,1)} %collective-permute-done.6), slice={[0:1152], [0:96]} | slice | bytes 442368 | tf_op jit(solution)/shard_map/slice | solution.py:153
  55.7 3.6 %collective-permute-start.7 = (bf16[1152,96]{0,1:T(8,128)(2,1)}, bf16[1152,96]{0,1:T(8,128)(2,1)}, u32[]{:S(2)}, u32[]{:S(2)}) collective-permute-start(bf16[1152,96]{0,1:T(8,128)(2,1)} %slice.24), channel_id=1, source_target_pairs={{0,16},{16,32},{32,48},{48,64},{64,80},{80,96},{96,112},{112,0},{1... | collective-permute-start | bytes 663560 | tf_op jit(solution)/shard_map/ppermute | solution.py:153
  59.2 0.0 copy-done
  59.3 0.2 constant_dynamic-slice_fusion
  59.4 0.2 copy.13
  59.6 0.0 all-to-all-done
  59.6 1.0 copy-done.5
  60.6 2.9 %strip_sums.2 = (f32[128,1024]{1,0:T(8,128)}, f32[128,1024]{1,0:T(8,128)S(1)}) custom-call(s32[1]{0:T(128)} %bitcast.core_ref, bf16[256,1152]{1,0:T(8,128)(2,1)S(1)} %bitcast.22, bf16[192,1152]{1,0:T(8,128)(2,1)S(1)} %bitcast.26, bf16[192,1152]{1,0:T(8,128)(2,1)S(1)} %bitcast.25, bf16[192,1152]{1,0:T(8,128)(2,1)S(1)} %bitcast.27, ...), custom_call_target="tpu_custom_call" | custom-call | flops 754974720 | bytes 4587520 | tf_op jit(solution)/shard_map/strip_sums/pallas_call | solution.py:58
  63.6 1.9 %collective-permute-start.4 = (f32[128,1024]{1,0:T(8,128)}, f32[128,1024]{1,0:T(8,128)S(1)}, u32[]{:S(2)}, u32[]{:S(2)}) collective-permute-start(f32[128,1024]{1,0:T(8,128)} %get-tuple-element.16), channel_id=1, source_target_pairs={{0,1},{1,0},{2,3},{3,2},{4,5},{5,4},{6,7},{7,6},{8,9},{9,8},{10,11... | collective-permute-start | bytes 1572872 | tf_op jit(solution)/shard_map/ppermute | solution.py:160
  65.5 0.0 collective-permute-done.8
  65.5 0.0 collective-permute-done.7
  65.5 2.2 %strip_sums.3 = (f32[128,640]{1,0:T(8,128)S(1)}, f32[128,640]{1,0:T(8,128)S(1)}) custom-call(s32[1]{0:T(128)} %bitcast.core_ref, bf16[256,1152]{1,0:T(8,128)(2,1)S(1)} %bitcast.23, bf16[192,1152]{1,0:T(8,128)(2,1)} %bitcast.8.refs_0_, bf16[96,1152]{1,0:T(8,128)(2,1)} %bitcast.9.refs_1_, bf16[96,1152]{1,0:T(8,128)(2,1)S(1)} %bitcast.29, ...), custom_call_target="tpu_custom_call" | custom-call | flops 528482304 | bytes 3309568 | tf_op jit(solution)/shard_map/strip_sums/pallas_call | solution.py:58
  67.7 2.4 %collective-permute-start.9 = (f32[128,640]{1,0:T(8,128)S(1)}, f32[128,640]{1,0:T(8,128)S(1)}, u32[]{:S(2)}, u32[]{:S(2)}) collective-permute-start(f32[128,640]{1,0:T(8,128)S(1)} %get-tuple-element.18), channel_id=1, source_target_pairs={{0,1},{1,0},{2,3},{3,2},{4,5},{5,4},{6,7},{7,6},{8,9},{9,8},{10,11... | collective-permute-start | bytes 983048 | tf_op jit(solution)/shard_map/ppermute | solution.py:160
  70.1 1.2 collective-permute-done.9
  71.4 0.2 reshape.31
  71.6 0.0 collective-permute-done.4
  71.6 0.1 add.25
  71.6 0.3 reshape.30
  72.0 1.3 %pad_maximum_fusion = f32[64,2,1664]{2,1,0:T(2,128)} fusion(f32[64,2,640]{2,1,0:T(2,128)S(1)} %reshape.31, f32[64,2,1024]{2,1,0:T(2,128)S(1)} %reshape.30), kind=kLoop, calls=%fused_computation | loop fusion | flops 212992 | bytes 1703936 | tf_op jit(solution)/shard_map/concatenate | solution.py:177
  73.3 23.2 %all-to-all-start.1 = ((f32[64,2,1664]{2,1,0:T(2,128)}), f32[64,2,1664]{2,1,0:T(2,128)}, u32[]{:S(2)}, u32[]{:S(2)}) async-start(f32[64,2,1664]{2,1,0:T(2,128)} %pad_maximum_fusion), calls=%async_computation.1 | async-start | bytes 1703936 | tf_op jit(solution)/shard_map/all_to_all | solution.py:164
  96.4 0.0 copy-start.1
  96.5 0.0 copy-start.6
  96.5 25.8 %all-to-all-done.1 = f32[64,2,1664]{2,1,0:T(2,128)} async-done(((f32[64,2,1664]{2,1,0:T(2,128)}), f32[64,2,1664]{2,1,0:T(2,128)}, u32[]{:S(2)}, u32[]{:S(2)}) %all-to-all-start.1) | async-done | bytes 852000 | tf_op jit(solution)/shard_map/all_to_all | solution.py:164
  122.3 1.5 %reduce_sum.9 = bf16[8,2,1664]{2,1,0:T(2,128)(2,1)S(1)} reduce(f32[8,8,2,1664]{3,2,1,0:T(2,128)} %bitcast.12, f32[]{:T(128)} %constant.55.clone.1), dimensions={0}, to_apply=%region_0.1 | reduce | flops 186368 | bytes 905220 | tf_op jit(solution)/shard_map/reduce_sum | solution.py:167
  123.8 0.1 slice.29
  123.9 0.1 concatenate.10
  124.0 0.1 reshape.33
  124.1 0.1 fusion
  124.2 0.1 reshape.34.queries_ref
  124.4 0.1 reshape.35.pairs_ref
  124.5 1.4 %attend.1 = bf16[2,48,256]{2,1,0:T(8,128)(2,1)S(1)} custom-call(s32[2]{0:T(128)S(1)} %copy-done.6, bf16[2,48,256]{2,1,0:T(8,128)(2,1)S(1)} %reshape.34.queries_ref, bf16[2,512]{1,0:T(2,128)(2,1)S(1)} %reshape.35.pairs_ref, bf16[2,1024,256]{2,1,0:T(8,128)(2,1)S(1)} %copy-done.1, bf16[2,1024,256]{2,1,0:T(8,128)(2,1)S(1)} %copy-done.2), custom_call_target="tpu_custom_call" | custom-call | flops 100663296 | bytes 2097152 | tf_op jit(solution)/shard_map/attend/pallas_call | solution.py:101
  125.9 0.7 copy.15
  (16 shorter events, 0.1 us)
Async XLA Ops:
  0.0 59.2 %copy-start = (bf16[1152,512]{1,0:T(8,128)(2,1)S(1)}, bf16[1152,512]{1,0:T(8,128)(2,1)}, u32[]{:S(2)}) copy-start(bf16[1152,512]{1,0:T(8,128)(2,1)} %param.8) | copy-start | bytes 3538948
  0.0 14.7 %collective-permute-start = (bf16[1152,192]{0,1:T(8,128)(2,1)}, bf16[1152,192]{0,1:T(8,128)(2,1)S(1)}, u32[]{:S(2)}, u32[]{:S(2)}) collective-permute-start(bf16[1152,192]{0,1:T(8,128)(2,1)} %param.7), channel_id=1, source_target_pairs={{0,16},{16,32},{32,48},{48,64},{64,80},{80,96},{96,112},{112,0},{1... | collective-permute-start | bytes 1327112 | tf_op jit(solution)/shard_map/ppermute | solution.py:141
  4.9 14.9 %collective-permute-start.1 = (bf16[1152,192]{0,1:T(8,128)(2,1)}, bf16[1152,192]{0,1:T(8,128)(2,1)S(1)}, u32[]{:S(2)}, u32[]{:S(2)}) collective-permute-start(bf16[1152,192]{0,1:T(8,128)(2,1)} %param.7), channel_id=1, source_target_pairs={{0,112},{16,0},{32,16},{48,32},{64,48},{80,64},{96,80},{112,96},{1... | collective-permute-start | bytes 1327112 | tf_op jit(solution)/shard_map/ppermute | solution.py:142
  19.9 35.8 %copy-start.4 = (bf16[1152,192]{0,1:T(8,128)(2,1)}, bf16[1152,192]{0,1:T(8,128)(2,1)S(1)}, u32[]{:S(2)}) copy-start(bf16[1152,192]{0,1:T(8,128)(2,1)S(1)} %collective-permute-done.1) | copy-start | bytes 1327108
  19.9 15.6 %collective-permute-start.2 = (bf16[1152,192]{0,1:T(8,128)(2,1)S(1)}, bf16[1152,192]{0,1:T(8,128)(2,1)}, u32[]{:S(2)}, u32[]{:S(2)}) collective-permute-start(bf16[1152,192]{0,1:T(8,128)(2,1)S(1)} %collective-permute-done.1), channel_id=1, source_target_pairs={{0,112},{16,0},{32,16},{48,32},{64,48},{80,64},{96,80},{112,96},{1... | collective-permute-start | bytes 1327112 | tf_op jit(solution)/shard_map/ppermute | solution.py:150
  21.8 17.7 %collective-permute-start.3 = (bf16[1152,192]{0,1:T(8,128)(2,1)S(1)}, bf16[1152,192]{0,1:T(8,128)(2,1)}, u32[]{:S(2)}, u32[]{:S(2)}) collective-permute-start(bf16[1152,192]{0,1:T(8,128)(2,1)S(1)} %collective-permute-done), channel_id=1, source_target_pairs={{0,16},{16,32},{32,48},{48,64},{64,80},{80,96},{96,112},{112,0},{1... | collective-permute-start | bytes 1327112 | tf_op jit(solution)/shard_map/ppermute | solution.py:149
  28.7 30.9 %all-to-all-start = ((bf16[8,32,1152]{2,1,0:T(8,128)(2,1)}), bf16[8,32,1152]{2,1,0:T(8,128)(2,1)S(1)}, u32[]{:S(2)}, u32[]{:S(2)}) async-start(bf16[8,32,1152]{2,1,0:T(8,128)(2,1)} %broadcast_in_dim.3), calls=%async_computation | async-start | bytes 1179648 | tf_op jit(solution)/shard_map/all_to_all | solution.py:145
  35.5 24.1 %copy-start.3 = (bf16[1152,192]{0,1:T(8,128)(2,1)S(1)}, bf16[1152,192]{0,1:T(8,128)(2,1)}, u32[]{:S(2)}) copy-start(bf16[1152,192]{0,1:T(8,128)(2,1)} %param.7) | copy-start | bytes 1327108
  35.5 13.4 %collective-permute-start.5 = (bf16[1152,192]{0,1:T(8,128)(2,1)}, bf16[1152,192]{0,1:T(8,128)(2,1)}, u32[]{:S(2)}, u32[]{:S(2)}) collective-permute-start(bf16[1152,192]{0,1:T(8,128)(2,1)} %collective-permute-done.2), channel_id=1, source_target_pairs={{0,112},{16,0},{32,16},{48,32},{64,48},{80,64},{96,80},{112,96},{1... | collective-permute-start | bytes 1327112 | tf_op jit(solution)/shard_map/ppermute | solution.py:150
  39.5 14.5 %collective-permute-start.6 = (bf16[1152,192]{0,1:T(8,128)(2,1)}, bf16[1152,192]{0,1:T(8,128)(2,1)}, u32[]{:S(2)}, u32[]{:S(2)}) collective-permute-start(bf16[1152,192]{0,1:T(8,128)(2,1)} %collective-permute-done.3), channel_id=1, source_target_pairs={{0,16},{16,32},{32,48},{48,64},{64,80},{80,96},{96,112},{112,0},{1... | collective-permute-start | bytes 1327112 | tf_op jit(solution)/shard_map/ppermute | solution.py:149
  50.5 15.0 %collective-permute-start.8 = (bf16[1152,96]{0,1:T(8,128)(2,1)}, bf16[1152,96]{0,1:T(8,128)(2,1)S(1)}, u32[]{:S(2)}, u32[]{:S(2)}) collective-permute-start(bf16[1152,96]{0,1:T(8,128)(2,1)} %slice.25), channel_id=1, source_target_pairs={{0,112},{16,0},{32,16},{48,32},{64,48},{80,64},{96,80},{112,96},{1... | collective-permute-start | bytes 663560 | tf_op jit(solution)/shard_map/ppermute | solution.py:154
  55.7 9.8 %collective-permute-start.7 = (bf16[1152,96]{0,1:T(8,128)(2,1)}, bf16[1152,96]{0,1:T(8,128)(2,1)}, u32[]{:S(2)}, u32[]{:S(2)}) collective-permute-start(bf16[1152,96]{0,1:T(8,128)(2,1)} %slice.24), channel_id=1, source_target_pairs={{0,16},{16,32},{32,48},{48,64},{64,80},{80,96},{96,112},{112,0},{1... | collective-permute-start | bytes 663560 | tf_op jit(solution)/shard_map/ppermute | solution.py:153
  59.6 1.0 copy-start.5
  63.6 8.0 %collective-permute-start.4 = (f32[128,1024]{1,0:T(8,128)}, f32[128,1024]{1,0:T(8,128)S(1)}, u32[]{:S(2)}, u32[]{:S(2)}) collective-permute-start(f32[128,1024]{1,0:T(8,128)} %get-tuple-element.16), channel_id=1, source_target_pairs={{0,1},{1,0},{2,3},{3,2},{4,5},{5,4},{6,7},{7,6},{8,9},{9,8},{10,11... | collective-permute-start | bytes 1572872 | tf_op jit(solution)/shard_map/ppermute | solution.py:160
  67.7 3.6 %collective-permute-start.9 = (f32[128,640]{1,0:T(8,128)S(1)}, f32[128,640]{1,0:T(8,128)S(1)}, u32[]{:S(2)}, u32[]{:S(2)}) collective-permute-start(f32[128,640]{1,0:T(8,128)S(1)} %get-tuple-element.18), channel_id=1, source_target_pairs={{0,1},{1,0},{2,3},{3,2},{4,5},{5,4},{6,7},{7,6},{8,9},{9,8},{10,11... | collective-permute-start | bytes 983048 | tf_op jit(solution)/shard_map/ppermute | solution.py:160
  73.3 51.2 %copy-start.2 = (bf16[2,1024,256]{2,1,0:T(8,128)(2,1)S(1)}, bf16[2,1024,256]{2,1,0:T(8,128)(2,1)}, u32[]{:S(2)}) copy-start(bf16[2,1024,256]{2,1,0:T(8,128)(2,1)} %values_ref.1) | copy-start | bytes 3145732
  73.3 49.0 %all-to-all-start.1 = ((f32[64,2,1664]{2,1,0:T(2,128)}), f32[64,2,1664]{2,1,0:T(2,128)}, u32[]{:S(2)}, u32[]{:S(2)}) async-start(f32[64,2,1664]{2,1,0:T(2,128)} %pad_maximum_fusion), calls=%async_computation.1 | async-start | bytes 1703936 | tf_op jit(solution)/shard_map/all_to_all | solution.py:164
  96.4 28.0 %copy-start.1 = (bf16[2,1024,256]{2,1,0:T(8,128)(2,1)S(1)}, bf16[2,1024,256]{2,1,0:T(8,128)(2,1)}, u32[]{:S(2)}) copy-start(bf16[2,1024,256]{2,1,0:T(8,128)(2,1)} %keys_ref.1) | copy-start | bytes 3145732
  96.5 28.0 %copy-start.6 = (s32[2]{0:T(128)S(1)}, s32[2]{0:T(128)}, u32[]{:S(2)}) copy-start(s32[2]{0:T(128)} %lengths_ref.1) | copy-start | bytes 28
